TPU v7x, 128 devices: a whole 4x4x4 slice. The times are simulated.
128 devices in a mesh: seg: 8 (over x, core), sec: 16 (over z, y).
Axes of the slice: x: 4, y: 4, z: 4, core: 2. Of those that a mesh axis runs over, the one named last changes fastest.
Arguments:
- psi: bfloat16 [8, 48, 128, 128], P('seg', 'sec'), may hold values from -600 to 600
- env_left: bfloat16 [8, 48, 40, 128, 128], P('seg', 'sec'), may hold values from -0.5 to 0.5
- env_right: bfloat16 [8, 48, 40, 128, 128], P('seg', 'sec'), may hold values from -0.5 to 0.5
- site_left: bfloat16 [8, 48, 128, 128], P('seg', 'sec'), may hold values from -0.5 to 0.5
- site_right: bfloat16 [8, 48, 128, 128], P('seg', 'sec'), may hold values from -0.5 to 0.5
- mix_left: float32 [8, 40, 40], P('seg'), may hold values from -1 to 1
- mix_right: float32 [8, 40, 40], P('seg'), may hold values from -1 to 1
- sources: int32 [8, 48, 6], P('seg', 'sec'), may hold values from 0 to 47
- terms: int32 [8, 48, 6], P('seg', 'sec'), may hold values from 0 to 7
- term_coef: float32 [8, 40], replicated, may hold values from -0.375 to 0.375
- energy: float32 [8, 48, 128], P('seg', 'sec'), may hold values from 0.5 to 4
Outputs:
- lanczos_vector: bfloat16 [8, 48, 128, 128], P('seg', 'sec')
- next_residual: float32 [8, 48, 128, 128], P('seg', 'sec')
- coefficients: float32 [8, 11], P('seg')
All inputs are finite; a program needn't handle non-finite values.
Results may differ from a plain program's by a relative error of at most 0.015.
Values may be sent and summed in bfloat16 or wider, within the bound.
A program may use at most 128 MiB of HBM per device.

v0:
```python
import jax
import jax.numpy as jnp
from jax import lax
from jax.sharding import PartitionSpec as P

APPS = 6


EPSILON = 1e-06
HIGH = lax.Precision.HIGHEST


def passed_along(value, axis, steps):
    count = lax.axis_size(axis)
    initial, last = (max(0, -steps), min(count, count - steps))
    return lax.ppermute(value, axis, [(source, source + steps) for source in range(initial, last)])


def premix(env, mix):
    return jnp.einsum("vw,bwij->bvij", mix, env.astype(jnp.float32), precision=HIGH).astype(
        jnp.bfloat16
    )


def sandwich(mixed, site):
    half = jnp.einsum("bvij,bjk->bvik", mixed, site, preferred_element_type=jnp.float32).astype(
        jnp.bfloat16
    )
    return jnp.einsum("bji,bvjk->bvik", site, half, preferred_element_type=jnp.float32).astype(
        jnp.bfloat16
    )


def apply_operator(vector, left_env, right_env, weights, sources, energy):
    piece = lax.all_gather(vector, "sec", axis=0, tiled=True)
    ids = jnp.arange(piece.shape[0], dtype=jnp.int32)
    hits = (sources[:, :, None] == ids[None, None, :]).astype(jnp.float32)
    select = jnp.einsum("tkw,tkb->twb", weights, hits, precision=HIGH)
    combo = jnp.einsum("twb,bij->twij", select, piece.astype(jnp.float32), precision=HIGH).astype(
        jnp.bfloat16
    )
    inner = jnp.einsum(
        "twij,twjk->twik", left_env, combo, preferred_element_type=jnp.float32
    ).astype(jnp.bfloat16)
    image = jnp.einsum("twik,twlk->til", inner, right_env, preferred_element_type=jnp.float32)
    return image + energy[:, :, None] * vector.astype(jnp.float32)


def on_device(
    psi,
    env_left,
    env_right,
    site_left,
    site_right,
    mix_left,
    mix_right,
    sources,
    terms,
    term_coef,
    energy,
):
    seg_index = lax.axis_index("seg")
    last_seg = lax.axis_size("seg") - 1
    own_left = env_left[0]
    own_right = env_right[0]
    grown_l = sandwich(premix(own_left, mix_left[0]), site_left[0])
    grown_r = sandwich(premix(own_right, mix_right[0]), site_right[0])
    arrived_l = passed_along(grown_l, "seg", 1)
    arrived_r = passed_along(grown_r, "seg", -1)
    left_env = jnp.where(seg_index == 0, own_left, arrived_l)
    right_env = jnp.where(seg_index == last_seg, own_right, arrived_r)
    kinds = term_coef.shape[0]
    kind_hits = (terms[0][:, :, None] == jnp.arange(kinds, dtype=jnp.int32)[None, None, :]).astype(
        jnp.float32
    )
    weights = jnp.einsum("tkm,mw->tkw", kind_hits, term_coef, precision=HIGH)
    block_sources = sources[0]
    block_energy = energy[0]
    vector = psi[0]
    count = float(vector.shape[0] * lax.axis_size("sec") * vector.shape[1] * vector.shape[2])
    start = vector.astype(jnp.float32)
    squares = lax.psum(jnp.sum(start * start), "sec")
    norm0 = jnp.sqrt(squares / count + EPSILON)
    first_vector = start / norm0
    image = (
        apply_operator(vector, left_env, right_env, weights, block_sources, block_energy) / norm0
    )
    alpha0 = lax.psum(jnp.sum(first_vector * image), "sec") / count
    rest = image - alpha0 * first_vector
    beta = jnp.sqrt(lax.psum(jnp.sum(rest * rest), "sec") / count + EPSILON)
    coefs = [alpha0, beta]
    previous = first_vector
    current = (rest / beta).astype(jnp.bfloat16)
    for step in range(1, APPS):
        image = apply_operator(current, left_env, right_env, weights, block_sources, block_energy)
        current_f = current.astype(jnp.float32)
        alpha = lax.psum(jnp.sum(current_f * image), "sec") / count
        rest = image - alpha * current_f - beta * previous
        coefs.append(alpha)
        if step < APPS - 1:
            beta = jnp.sqrt(lax.psum(jnp.sum(rest * rest), "sec") / count + EPSILON)
            coefs.append(beta)
            previous = current_f
            current = (rest / beta).astype(jnp.bfloat16)
    return (current[None], rest[None], jnp.stack(coefs)[None])


def solution(mesh):
    in_specs = (
        P("seg", "sec", None, None),
        P("seg", "sec", None, None, None),
        P("seg", "sec", None, None, None),
        P("seg", "sec", None, None),
        P("seg", "sec", None, None),
        P("seg", None, None),
        P("seg", None, None),
        P("seg", "sec", None),
        P("seg", "sec", None),
        P(),
        P("seg", "sec", None),
    )
    out_specs = (P("seg", "sec", None, None), P("seg", "sec", None, None), P("seg", None))
    return jax.shard_map(
        on_device, mesh=mesh, in_specs=in_specs, out_specs=out_specs, check_vma=False
    )
```

profile of v0, /device:TPU:0, one launch (start us, length us, event | category | flops | bytes accessed | tf_op | source)
XLA Modules:
  0.0 838.8 jit_solution(10378513404993418211)
XLA Ops:
  7.2 8.6 %convert_bitcast_fusion.1 = bf16[3,40,128,128]{3,1,2,0:T(8,128)(2,1)} fusion(bf16[3,40,128,128]{3,2,1,0:T(8,128)(2,1)} %bitcast.159, f32[1,40,40]{2,1,0:T(8,128)} %param.17), kind=kOutput, calls=%fused_computation.35 | convolution fusion | flops 945684480 | bytes 7870720 | tf_op jit(solution)/shard_map/vw,bwij->bvij/dot_general | solution.py:20
  23.5 8.7 %convert_bitcast_fusion.3 = bf16[3,40,128,128]{3,1,2,0:T(8,128)(2,1)} fusion(bf16[3,40,128,128]{3,2,1,0:T(8,128)(2,1)} %bitcast.160, f32[1,40,40]{2,1,0:T(8,128)S(1)} %copy-done.10), kind=kOutput, calls=%fused_computation.41 | convolution fusion | flops 945684480 | bytes 7870720 | tf_op jit(solution)/shard_map/vw,bwij->bvij/dot_general | solution.py:20
  44.2 42.9 %psum.84 = f32[]{:T(128)} all-reduce(f32[]{:T(128)} %fusion.161), channel_id=1, replica_groups=mesh['seg'=8,'sec'=16] {'sec'}, use_global_device_ids=true, to_apply=%region_1.2 | all-reduce | flops 1 | bytes 8 | tf_op jit(solution)/shard_map/psum | solution.py:82
  93.4 6.4 copy.31
  101.1 6.8 convolution_convert_fusion.5
  114.7 7.6 multiply_reduce_fusion.5
  122.3 36.1 %psum.85 = f32[]{:T(128)} all-reduce(f32[]{:T(128)} %get-tuple-element.3), channel_id=1, replica_groups=mesh['seg'=8,'sec'=16] {'sec'}, use_global_device_ids=true, to_apply=%region_3.4 | all-reduce | flops 1 | bytes 8 | tf_op jit(solution)/shard_map/psum | solution.py:88
  159.7 38.1 %psum.86 = f32[]{:T(128)} all-reduce(f32[]{:T(128)} %multiply_reduce_fusion.4), channel_id=1, replica_groups=mesh['seg'=8,'sec'=16] {'sec'}, use_global_device_ids=true, to_apply=%region_5.6 | all-reduce | flops 1 | bytes 8 | tf_op jit(solution)/shard_map/psum | solution.py:90
  199.4 42.0 %all-gather.8.cloned.1.call-done = bf16[48,128,128]{2,1,0:T(8,128)(2,1)} async-done(((bf16[3,128,128]{2,1,0:T(8,128)(2,1)}), bf16[48,128,128]{2,1,0:T(8,128)(2,1)}) %all-gather.8.cloned.1.call-update) | async-done | bytes 1572880 | tf_op jit(solution)/shard_map/all_gather | solution.py:35
  241.5 6.7 convolution_convert_fusion.4
  248.2 7.6 fusion.162
  255.7 38.7 %psum.87 = f32[]{:T(128)} all-reduce(f32[]{:T(128)} %get-tuple-element.5), channel_id=1, replica_groups=mesh['seg'=8,'sec'=16] {'sec'}, use_global_device_ids=true, to_apply=%region_7.8 | all-reduce | flops 1 | bytes 8 | tf_op jit(solution)/shard_map/psum | solution.py:97
  295.8 36.1 %psum.88 = f32[]{:T(128)} all-reduce(f32[]{:T(128)} %multiply_reduce_fusion.3), channel_id=1, replica_groups=mesh['seg'=8,'sec'=16] {'sec'}, use_global_device_ids=true, to_apply=%region_9.10 | all-reduce | flops 1 | bytes 8 | tf_op jit(solution)/shard_map/psum | solution.py:101
  333.6 41.6 %all-gather.10.cloned.1.call-done = bf16[48,128,128]{2,1,0:T(8,128)(2,1)} async-done(((bf16[3,128,128]{2,1,0:T(8,128)(2,1)}), bf16[48,128,128]{2,1,0:T(8,128)(2,1)}) %all-gather.10.cloned.1.call-update) | async-done | bytes 1572880 | tf_op jit(solution)/shard_map/all_gather | solution.py:35
  375.2 6.7 convolution_convert_fusion.3
  381.9 7.6 fusion.166
  389.5 38.7 %psum.89 = f32[]{:T(128)} all-reduce(f32[]{:T(128)} %get-tuple-element.7), channel_id=1, replica_groups=mesh['seg'=8,'sec'=16] {'sec'}, use_global_device_ids=true, to_apply=%region_11.12 | all-reduce | flops 1 | bytes 8 | tf_op jit(solution)/shard_map/psum | solution.py:97
  429.5 36.1 %psum.90 = f32[]{:T(128)} all-reduce(f32[]{:T(128)} %multiply_reduce_fusion.2), channel_id=1, replica_groups=mesh['seg'=8,'sec'=16] {'sec'}, use_global_device_ids=true, to_apply=%region_13.14 | all-reduce | flops 1 | bytes 8 | tf_op jit(solution)/shard_map/psum | solution.py:101
  467.6 41.4 %all-gather.12.cloned.1.call-done = bf16[48,128,128]{2,1,0:T(8,128)(2,1)} async-done(((bf16[3,128,128]{2,1,0:T(8,128)(2,1)}), bf16[48,128,128]{2,1,0:T(8,128)(2,1)}) %all-gather.12.cloned.1.call-update) | async-done | bytes 1572880 | tf_op jit(solution)/shard_map/all_gather | solution.py:35
  509.0 6.7 convolution_convert_fusion.2
  515.7 7.6 fusion.169
  523.2 38.7 %psum.91 = f32[]{:T(128)} all-reduce(f32[]{:T(128)} %get-tuple-element.9), channel_id=1, replica_groups=mesh['seg'=8,'sec'=16] {'sec'}, use_global_device_ids=true, to_apply=%region_15.16 | all-reduce | flops 1 | bytes 8 | tf_op jit(solution)/shard_map/psum | solution.py:97
  563.3 36.1 %psum.92 = f32[]{:T(128)} all-reduce(f32[]{:T(128)} %multiply_reduce_fusion.1), channel_id=1, replica_groups=mesh['seg'=8,'sec'=16] {'sec'}, use_global_device_ids=true, to_apply=%region_17.18 | all-reduce | flops 1 | bytes 8 | tf_op jit(solution)/shard_map/psum | solution.py:101
  601.0 41.7 %all-gather.14.cloned.1.call-done = bf16[48,128,128]{2,1,0:T(8,128)(2,1)} async-done(((bf16[3,128,128]{2,1,0:T(8,128)(2,1)}), bf16[48,128,128]{2,1,0:T(8,128)(2,1)}) %all-gather.14.cloned.1.call-update) | async-done | bytes 1572880 | tf_op jit(solution)/shard_map/all_gather | solution.py:35
  642.7 6.7 convolution_convert_fusion.1
  649.4 7.6 fusion.172
  657.0 38.7 %psum.93 = f32[]{:T(128)} all-reduce(f32[]{:T(128)} %get-tuple-element.11), channel_id=1, replica_groups=mesh['seg'=8,'sec'=16] {'sec'}, use_global_device_ids=true, to_apply=%region_19.20 | all-reduce | flops 1 | bytes 8 | tf_op jit(solution)/shard_map/psum | solution.py:97
  697.0 36.3 %psum.94 = f32[]{:T(128)} all-reduce(f32[]{:T(128)} %multiply_reduce_fusion), channel_id=1, replica_groups=mesh['seg'=8,'sec'=16] {'sec'}, use_global_device_ids=true, to_apply=%region_21.22 | all-reduce | flops 1 | bytes 8 | tf_op jit(solution)/shard_map/psum | solution.py:101
  734.7 41.9 %all-gather.16.cloned.1.call-done = bf16[48,128,128]{2,1,0:T(8,128)(2,1)} async-done(((bf16[3,128,128]{2,1,0:T(8,128)(2,1)}), bf16[48,128,128]{2,1,0:T(8,128)(2,1)}) %all-gather.16.cloned.1.call-update) | async-done | bytes 1572880 | tf_op jit(solution)/shard_map/all_gather | solution.py:35
  776.7 6.7 convolution_convert_fusion
  783.4 7.6 fusion.157
  791.0 38.7 %psum.95 = f32[]{:T(128)} all-reduce(f32[]{:T(128)} %get-tuple-element.13), channel_id=1, replica_groups=mesh['seg'=8,'sec'=16] {'sec'}, use_global_device_ids=true, to_apply=%region_23.24 | all-reduce | flops 1 | bytes 8 | tf_op jit(solution)/shard_map/psum | solution.py:97
  (72 shorter events, 43.1 us)
Async XLA Ops:
  7.2 8.6 %copy-start = (bf16[1,3,128,128]{3,2,1,0:T(8,128)(2,1)S(1)}, bf16[1,3,128,128]{3,2,1,0:T(8,128)(2,1)}, u32[]{:S(2)}) copy-start(bf16[1,3,128,128]{3,2,1,0:T(8,128)(2,1)} %param.15) | copy-start | bytes 294916
  7.2 93.9 %all-gather.18.cloned.1.call-start = ((), (), s32[]{:S(2)}) async-start(), calls=%async_computation.5 | async-start | bytes 1671168 | tf_op jit(solution)/shard_map/all_gather | solution.py:35
  15.8 7.7 copy-start.10
  22.0 85.8 %collective-permute-start.1 = (bf16[3,40,128,128]{2,3,1,0:T(8,128)(2,1)}, bf16[3,40,128,128]{2,3,1,0:T(8,128)(2,1)}, u32[]{:S(2)}, u32[]{:S(2)}) collective-permute-start(bf16[3,40,128,128]{2,3,1,0:T(8,128)(2,1)} %convert_bitcast_fusion), channel_id=1, source_target_pairs={{16,0},{32,16},{48,32},{64,48},{80,64},{96,80},{112,96},{17,1},{33... | collective-permute-start | bytes 11796488 | tf_op jit(solution)/shard_map/ppermute | solution.py:16
  23.5 8.7 %copy-start.14 = (bf16[1,3,128,128]{3,2,1,0:T(8,128)(2,1)S(1)}, bf16[1,3,128,128]{3,2,1,0:T(8,128)(2,1)}, u32[]{:S(2)}) copy-start(bf16[1,3,128,128]{3,2,1,0:T(8,128)(2,1)} %param.14) | copy-start | bytes 294916
  32.2 11.4 %copy-start.4 = (bf16[1,3,128,128]{3,2,1,0:T(8,128)(2,1)S(1)}, bf16[1,3,128,128]{3,2,1,0:T(8,128)(2,1)}, u32[]{:S(2)}) copy-start(bf16[1,3,128,128]{3,2,1,0:T(8,128)(2,1)} %param.11) | copy-start | bytes 294916
  38.5 73.9 %collective-permute-start = (bf16[3,40,128,128]{2,3,1,0:T(8,128)(2,1)}, bf16[3,40,128,128]{2,3,1,0:T(8,128)(2,1)}, u32[]{:S(2)}, u32[]{:S(2)}) collective-permute-start(bf16[3,40,128,128]{2,3,1,0:T(8,128)(2,1)} %convert_bitcast_fusion.2), channel_id=1, source_target_pairs={{0,16},{16,32},{32,48},{48,64},{64,80},{80,96},{96,112},{1,17},{17... | collective-permute-start | bytes 11796488 | tf_op jit(solution)/shard_map/ppermute | solution.py:16
  43.5 197.9 %all-gather.8.cloned.1.call-start = ((), (), s32[]{:S(2)}) async-start(), calls=%async_computation | async-start | bytes 1671168 | tf_op jit(solution)/shard_map/all_gather | solution.py:35
  93.4 6.4 copy-start.11
  93.4 6.4 copy-start.12
  93.4 6.4 copy-start.13
  93.4 7.1 copy-start.15
  101.1 6.8 copy-start.3
  107.8 4.6 copy-start.2
  199.1 49.0 %copy-start.7 = (bf16[3,128,128]{2,1,0:T(8,128)(2,1)S(1)}, bf16[3,128,128]{2,1,0:T(8,128)(2,1)}, u32[]{:S(2)}) copy-start(bf16[3,128,128]{2,1,0:T(8,128)(2,1)} %divide_convert_fusion.4) | copy-start | bytes 294916
  199.1 176.1 %all-gather.10.cloned.1.call-start = ((), (), s32[]{:S(2)}) async-start(), calls=%async_computation.1 | async-start | bytes 1671168 | tf_op jit(solution)/shard_map/all_gather | solution.py:35
  333.3 48.7 %copy-start.6 = (bf16[3,128,128]{2,1,0:T(8,128)(2,1)S(1)}, bf16[3,128,128]{2,1,0:T(8,128)(2,1)}, u32[]{:S(2)}) copy-start(bf16[3,128,128]{2,1,0:T(8,128)(2,1)} %divide_convert_fusion.3) | copy-start | bytes 294916
  333.3 175.7 %all-gather.12.cloned.1.call-start = ((), (), s32[]{:S(2)}) async-start(), calls=%async_computation.2 | async-start | bytes 1671168 | tf_op jit(solution)/shard_map/all_gather | solution.py:35
  467.0 48.7 %copy-start.5 = (bf16[3,128,128]{2,1,0:T(8,128)(2,1)S(1)}, bf16[3,128,128]{2,1,0:T(8,128)(2,1)}, u32[]{:S(2)}) copy-start(bf16[3,128,128]{2,1,0:T(8,128)(2,1)} %divide_convert_fusion.2) | copy-start | bytes 294916
  467.0 175.7 %all-gather.14.cloned.1.call-start = ((), (), s32[]{:S(2)}) async-start(), calls=%async_computation.3 | async-start | bytes 1671168 | tf_op jit(solution)/shard_map/all_gather | solution.py:35
  600.8 48.7 %copy-start.8 = (bf16[3,128,128]{2,1,0:T(8,128)(2,1)S(1)}, bf16[3,128,128]{2,1,0:T(8,128)(2,1)}, u32[]{:S(2)}) copy-start(bf16[3,128,128]{2,1,0:T(8,128)(2,1)} %divide_convert_fusion.1) | copy-start | bytes 294916
  600.8 175.9 %all-gather.16.cloned.1.call-start = ((), (), s32[]{:S(2)}) async-start(), calls=%async_computation.4 | async-start | bytes 1671168 | tf_op jit(solution)/shard_map/all_gather | solution.py:35
  734.7 48.7 %copy-start.9 = (bf16[3,128,128]{2,1,0:T(8,128)(2,1)S(1)}, bf16[3,128,128]{2,1,0:T(8,128)(2,1)}, u32[]{:S(2)}) copy-start(bf16[3,128,128]{2,1,0:T(8,128)(2,1)} %divide_convert_fusion) | copy-start | bytes 294916
  776.7 55.0 %copy-start.1 = (bf16[1,3,128,128]{3,2,1,0:T(8,128)(2,1)S(1)}, bf16[1,3,128,128]{3,2,1,0:T(8,128)(2,1)}, u32[]{:S(2)}) copy-start(bf16[1,3,128,128]{3,2,1,0:T(8,128)(2,1)} %param.15) | copy-start | bytes 294916
Sparse Core Ops, SparseCore 0:
  43.6 46.1 all-gather.17
  199.3 42.1 all-gather.7
  333.4 41.7 all-gather.9
  467.2 41.7 all-gather.11
  600.9 41.7 all-gather.13
  734.9 41.7 all-gather.15
where the time goes:
time: 845 us; the launch traced here: 839 us
  blocking collectives  455 us (54%)
  waiting for transfers between devices  209 us (25%)
  matrix products  116 us (14%)
  between operations  22.6 us (3%)
  other arithmetic  15 us (2%)
  local copies, waits for them, and re-layouts  13.4 us (2%)
    all_gather x6, waiting for transfers between devices, apply_operator(): piece = lax.all_gather(vector, 'sec', axis=0, tiled=True)  209 us
    psum x5, blocking collectives, on_device(): alpha = lax.psum(jnp.sum(current_f * image), 'sec') / count  194 us
    psum x5, blocking collectives, on_device(): beta = jnp.sqrt(lax.psum(jnp.sum(rest * rest), 'sec') / count + EPSILON)  183 us
    dot_general x6, matrix products, apply_operator(): jnp.einsum('twik,twlk->til', inner, right_env, preferred_element_type=jnp...  45.4 us
    psum x1, blocking collectives, on_device(): squares = lax.psum(jnp.sum(start * start), 'sec')  42.9 us
    dot_general x6, matrix products, apply_operator(): jnp.einsum('twb,bij->twij', select, piece.astype(jnp.float32), precision=...  40.3 us
    psum x1, blocking collectives, on_device(): alpha0 = lax.psum(jnp.sum(first_vector * image), 'sec') / count  36.1 us
    dot_general x2, matrix products, premix(): jnp.einsum('vw,bwij->bvij', mix, env.astype(jnp.float32), precision=HIGH)  17.3 us
  transfers between devices with their start and end apart: 8, of which 5 were waited for; matrix products, arithmetic and copies ran while one was open for 5% of the time, Pallas kernels for 0%

commit v1 on v0

v1 whole, which is shorter than its diff:
```python
import functools

import jax
import jax.numpy as jnp
from jax import lax
from jax.experimental import pallas as pl
from jax.experimental.pallas import tpu as pltpu
from jax.sharding import PartitionSpec as P

APPS = 6
EPSILON = 1e-06
CH = 40
BD = 128
ENT = 6
BLK = 3
HALF = BD // 2
TILE = 16
MESH = pl.DeviceIdType.MESH
BF = jnp.bfloat16
F32 = jnp.float32

CHUNK = 8
CHUNKS = CH // CHUNK
GROUPS = ((0, 3),)


def dot(a, b):
    return lax.dot_general(a, b, (((1,), (0,)), ((), ())), preferred_element_type=F32)


def dot_nt(a, b):
    return lax.dot_general(a, b, (((1,), (1,)), ((), ())), preferred_element_type=F32)


def total(x):
    lanes = jnp.sum(x, axis=0, keepdims=True)
    return jnp.broadcast_to(jnp.sum(lanes, axis=1, keepdims=True), (1, BD))


def split(x):
    high = x.astype(BF)
    return high, (x - high.astype(F32)).astype(BF)


def wait_bytes(ref, sem):
    pltpu.make_async_copy(ref, ref, sem).wait()


def spread(rows, start):
    row = lax.broadcasted_iota(jnp.int32, (rows, CH), 0) + start
    return (row // TILE == lax.broadcasted_iota(jnp.int32, (rows, CH), 1)).astype(BF)


def same_state(rows, cols):
    row = lax.broadcasted_iota(jnp.int32, (rows, cols), 0)
    col = lax.broadcasted_iota(jnp.int32, (rows, cols), 1)
    return row % TILE == col % TILE


def kernel(
    segs,
    count,
    psi,
    env_left,
    env_right,
    site_left,
    site_right,
    mix_left,
    mix_right,
    sources,
    terms,
    term_coef,
    energy,
    out_vector,
    out_rest,
    out_coef,
    env_in,
    grown,
    envs,
    mixed,
    mix_kron,
    site_t,
    term_kron,
    combo,
    image,
    on_site,
    picked,
    own,
    before,
    leftover,
    half0,
    half1,
    stats,
    local0,
    local1,
    local_stats,
    place,
    load_sem,
    env_send,
    env_recv,
    s1,
    r1,
    s2,
    r2,
    stat_send,
    stat_recv,
):
    seg = lax.axis_index("seg")
    sec = lax.axis_index("sec")
    my_z = sec // 4
    my_y = sec % 4

    def along_z(d):
        return (seg, ((my_z + d) % 4) * 4 + my_y)

    def along_y(d):
        return (seg, my_z * 4 + (my_y + d) % 4)

    def send(src, dst, ssem, rsem, device):
        pltpu.make_async_remote_copy(
            src_ref=src, dst_ref=dst, send_sem=ssem, recv_sem=rsem,
            device_id=device, device_id_type=MESH,
        ).start()

    loads = []
    for b in range(BLK):
        for side, ref in ((0, env_left), (1, env_right)):
            c = pltpu.make_async_copy(ref.at[b], env_in.at[side, b], load_sem.at[side, b])
            c.start()
            loads.append(c)

    barrier = pltpu.get_barrier_semaphore()
    for d in (1, 2, 3):
        pl.semaphore_signal(barrier, inc=1, device_id=along_z(d), device_id_type=MESH)
        pl.semaphore_signal(barrier, inc=1, device_id=along_y(d), device_id_type=MESH)

    @pl.when(seg > 0)
    def _():
        pl.semaphore_signal(barrier, inc=1, device_id=(seg - 1, sec), device_id_type=MESH)

    @pl.when(seg < segs - 1)
    def _():
        pl.semaphore_signal(barrier, inc=1, device_id=(seg + 1, sec), device_id_type=MESH)

    def end_copy(side):
        source = env_left if side == 0 else env_right
        return pltpu.make_async_copy(source, envs.at[side], load_sem.at[side, BLK])

    @pl.when(seg == 0)
    def _():
        end_copy(0).start()

    @pl.when(seg == segs - 1)
    def _():
        end_copy(1).start()

    for side, ref in ((0, mix_left), (1, mix_right)):
        for part, mix in enumerate(split(ref[...])):
            def build(m, _, side=side, part=part, mix=mix):
                rows = dot(spread(BD, m * BD), mix).astype(BF)
                full = dot_nt(rows, spread(CH * TILE, 0))
                keep = same_state(BD, CH * TILE)
                at = pl.ds(pl.multiple_of(m * BD, BD), BD)
                mix_kron[side, part, at, :] = jnp.where(keep, full, 0.0).astype(BF)
                return 0

            lax.fori_loop(0, CH * TILE // BD, build, 0)

    eye_row = lax.broadcasted_iota(jnp.int32, (BD, BD), 0)
    eye = (eye_row == lax.broadcasted_iota(jnp.int32, (BD, BD), 1)).astype(BF)
    for side, ref in ((0, site_left), (1, site_right)):
        for b in range(BLK):
            site_t[side, b] = dot_nt(eye, ref[b]).astype(BF)

    for p in range(2):
        stats[p, 0, 0] = jnp.zeros((2, 8, BD), F32)
    for t in range(BLK):
        half0[0, t, 0, 0] = psi[t, :HALF, :]
        half1[0, t, 0, 0] = psi[t, HALF:, :]
        own[t] = psi[t]

    pl.semaphore_wait(
        barrier, 6 + jnp.where(seg > 0, 1, 0) + jnp.where(seg < segs - 1, 1, 0)
    )

    def gather_first(p, g):
        ts = pl.ds(*GROUPS[g])
        for d in (1, 3, 2):
            back = (4 - d) % 4
            send(half0.at[p, ts, 0, 0], half0.at[p, ts, 0, back], s1.at[p, g, 0], r1.at[p, g, 0], along_z(d))
            send(half1.at[p, ts, 0, 0], half1.at[p, ts, 0, back], s1.at[p, g, 1], r1.at[p, g, 1], along_y(d))

    def gather_second(p, g):
        ts = pl.ds(*GROUPS[g])
        for h, ref, along in ((0, half0, along_y), (1, half1, along_z)):
            wait_bytes(ref.at[p, ts, 0, pl.ds(1, 3)], r1.at[p, g, h])
            for d in (1, 3, 2):
                back = (4 - d) % 4
                send(ref.at[p, ts, 0], ref.at[p, ts, back], s2.at[p, g, h], r2.at[p, g, h], along(d))

    def gather_end(p):
        for g, group in enumerate(GROUPS):
            ts = pl.ds(*group)
            for h, ref in ((0, half0), (1, half1)):
                wait_bytes(ref.at[p, ts, pl.ds(1, 3)], r2.at[p, g, h])
                wait_bytes(ref.at[p, ts, 0, pl.ds(1, 3)], s1.at[p, g, h])
                wait_bytes(ref.at[p, ts, pl.ds(1, 3)], s2.at[p, g, h])

    def stats_first(p):
        for d in (1, 3, 2):
            send(stats.at[p, 0, 0], stats.at[p, 0, (4 - d) % 4], stat_send.at[p, 0], stat_recv.at[p, 0], along_z(d))

    def stats_second(p):
        wait_bytes(stats.at[p, 0, pl.ds(1, 3)], stat_recv.at[p, 0])
        for d in (1, 3, 2):
            send(stats.at[p, 0], stats.at[p, (4 - d) % 4], stat_send.at[p, 1], stat_recv.at[p, 1], along_y(d))

    def stats_end(p):
        wait_bytes(stats.at[p, pl.ds(1, 3)], stat_recv.at[p, 1])
        wait_bytes(stats.at[p, 0, pl.ds(1, 3)], stat_send.at[p, 0])
        wait_bytes(stats.at[p, pl.ds(1, 3)], stat_send.at[p, 1])

    for g in range(len(GROUPS)):
        gather_first(0, g)

    def env_copy(side, b, c):
        part = pl.ds(c * CHUNK, CHUNK)
        to = seg + 1 if side == 0 else seg - 1
        return pltpu.make_async_remote_copy(
            src_ref=grown.at[side, b, part],
            dst_ref=envs.at[side, b, part],
            send_sem=env_send.at[side, b, c],
            recv_sem=env_recv.at[side, b, c],
            device_id=(to, sec),
            device_id_type=MESH,
        )

    def grow(step, _):
        b = step // CHUNKS
        c = step % CHUNKS
        for side, site in ((0, site_left), (1, site_right)):
            @pl.when(c == 0)
            def _(side=side):
                wait_bytes(env_in.at[side, b], load_sem.at[side, b])

            rows = pl.ds(pl.multiple_of(c * CHUNK * TILE, CHUNK * TILE), CHUNK * TILE)
            high = mix_kron[side, 0, rows, :]
            low = mix_kron[side, 1, rows, :]
            for i in range(BD // (2 * TILE)):
                base = i * 2 * TILE
                cols = [
                    env_in[side, b, :, base + h * TILE:base + (h + 1) * TILE, :].reshape(CH * TILE, BD)
                    for h in range(2)
                ]
                both = jnp.concatenate(cols, axis=1)
                out = (dot(high, both) + dot(low, both)).astype(BF)
                for h in range(2):
                    mixed[:, base + h * TILE:base + (h + 1) * TILE, :] = out[:, h * BD:(h + 1) * BD].reshape(
                        CHUNK, TILE, BD
                    )
            half = dot(mixed[...].reshape(CHUNK * BD, BD), site[b]).astype(BF)
            wide = jnp.concatenate([half[v * BD:(v + 1) * BD] for v in range(CHUNK)], axis=1)
            done = dot(site_t[side, b], wide).astype(BF)
            for v in range(CHUNK):
                grown[side, b, c * CHUNK + v] = done[:, v * BD:(v + 1) * BD]

            @pl.when(seg < segs - 1 if side == 0 else seg > 0)
            def _(side=side):
                env_copy(side, b, c).start()

        return 0

    lax.fori_loop(0, BLK * CHUNKS, grow, 0)

    for g in range(len(GROUPS)):
        gather_second(0, g)

    for t in range(BLK):
        row = jnp.broadcast_to(energy[t:t + 1, :], (BD, BD))
        on_site[t] = jnp.transpose(row)
    spread_all = spread(CH * TILE, 0)
    keep = same_state(CH * TILE, ENT * TILE)
    for t in range(BLK):
        entry = lax.broadcasted_iota(jnp.int32, (8, ENT * TILE), 1) // TILE
        kind = jnp.zeros((8, ENT * TILE), jnp.int32)
        for k in range(ENT):
            kind = jnp.where(entry == k, terms[t, k], kind)
        hit = (kind == lax.broadcasted_iota(jnp.int32, (8, ENT * TILE), 0)).astype(BF)
        for part, coef in enumerate(split(term_coef[...])):
            rows = dot_nt(spread_all, coef).astype(BF)
            full = dot(rows, hit)
            term_kron[t, :, part * ENT * TILE:(part + 1) * ENT * TILE] = jnp.where(keep, full, 0.0).astype(BF)

    def where_is(t, k):
        s = sources[t, k]
        owner = s // BLK
        sub = s - BLK * owner
        return sub, (owner % 4 - my_y + 4) % 4, (owner // 4 - my_z + 4) % 4

    for t in range(BLK):
        for k in range(ENT):
            for n, value in enumerate(where_is(t, k)):
                place[n, t * ENT + k] = value

    gather_end(0)

    local0[...] = half0[0]
    local1[...] = half1[0]

    def fetch(q, _):
        sub, y, z = place[0, q], place[1, q], place[2, q]
        picked[q, :HALF, :] = local0[sub, y, z]
        picked[q, HALF:, :] = local1[sub, z, y]
        return 0

    lax.fori_loop(0, BLK * ENT, fetch, 0)

    def squares(n, acc):
        t, o = n // 4, n % 4
        for i in range(4):
            for ref in (half0, half1):
                x = ref[0, t, o, i].astype(F32)
                acc = acc + x * x
        return acc

    norm = total(lax.fori_loop(0, BLK * 4, squares, jnp.zeros((HALF, BD), F32)))
    sigma0 = 1.0 / jnp.sqrt(norm / count + EPSILON)

    def combine(t):
        for i in range(BD // (2 * TILE)):
            base = i * 2 * TILE
            cols = [
                picked[t * ENT:(t + 1) * ENT, base + h * TILE:base + (h + 1) * TILE, :].reshape(ENT * TILE, BD)
                for h in range(2)
            ]
            both = jnp.concatenate(cols, axis=1)
            out = dot(term_kron[t], jnp.concatenate([both, both], axis=0)).astype(BF)
            for h in range(2):
                combo[t, :, base + h * TILE:base + (h + 1) * TILE, :] = out[:, h * BD:(h + 1) * BD].reshape(
                    CH, TILE, BD
                )

    def contract(t, first, n):
        inner = [dot(envs[0, t, first + j], combo[t, first + j]).astype(BF) for j in range(n)]
        right = [envs[1, t, first + j] for j in range(n)]
        return dot_nt(jnp.concatenate(inner, axis=1), jnp.concatenate(right, axis=1))

    def finish(p, t, applied, sigma, beta):
        v = own[t].astype(F32) * sigma
        img = applied * sigma + on_site[t] * v
        w = img if beta is None else img - beta * before[t]
        prod = total(img * v)
        norm = total(v * v)
        over = total(w * v)
        a = jnp.where(norm > 0.0, over / jnp.where(norm > 0.0, norm, 1.0), 0.0)
        y = w - a * v
        leftover[t] = y
        low = y.astype(BF)
        half0[p, t, 0, 0] = low[:HALF]
        half1[p, t, 0, 0] = low[HALF:]
        stats[p, 0, 0, 0, t:t + 1, :] = prod
        stats[p, 0, 0, 0, 4 + t:5 + t, :] = norm
        stats[p, 0, 0, 1, t:t + 1, :] = a
        stats[p, 0, 0, 1, 4 + t:5 + t, :] = total(y * y)

    def scalars(p):
        def add(x):
            lines = jnp.sum(x.reshape(16, 4, BD), axis=0)
            return jnp.sum(lines, axis=0, keepdims=True)

        alpha = add(stats[p, :, :, 0, 0:4, :]) / count
        gap = alpha - stats[p, :, :, 1, 0:4, :]
        squared = stats[p, :, :, 1, 4:8, :] + gap * gap * stats[p, :, :, 0, 4:8, :]
        return alpha, jnp.sqrt(add(squared) / count + EPSILON)

    for t in range(BLK):
        combine(t)

    @pl.when(seg == 0)
    def _():
        end_copy(0).wait()

    @pl.when(seg == segs - 1)
    def _():
        end_copy(1).wait()

    image[...] = jnp.zeros_like(image)

    def apply_first(step, _):
        b = step // CHUNKS
        c = step % CHUNKS

        @pl.when(seg > 0)
        def _():
            env_copy(0, b, c).wait_recv()

        @pl.when(seg < segs - 1)
        def _():
            env_copy(1, b, c).wait_recv()

        image[b] = image[b] + contract(b, c * CHUNK, CHUNK)
        return 0

    lax.fori_loop(0, BLK * CHUNKS, apply_first, 0)
    for t in range(BLK):
        finish(1, t, image[t], sigma0, None)
    for g in range(len(GROUPS)):
        gather_first(1, g)
    stats_first(1)
    stats_second(1)
    for g in range(len(GROUPS)):
        gather_second(1, g)

    lane = lax.broadcasted_iota(jnp.int32, (1, BD), 1)

    def application(k, carry):
        coefs, sigma = carry
        last = k % 2
        p = (k + 1) % 2
        stats_end(last)
        alpha, beta = scalars(last)
        coefs = jnp.where(lane == 2 * k - 2, alpha, coefs)
        coefs = jnp.where(lane == 2 * k - 1, beta, coefs)
        inverse = 1.0 / beta
        local_stats[...] = stats[last, :, :, 1]
        gather_end(last)
        local0[...] = half0[last]
        local1[...] = half1[last]

        for t in range(BLK):
            gap = (alpha - stats[last, 0, 0, 1, t:t + 1, :]) * sigma
            v = own[t].astype(F32)
            before[t] = v * sigma
            for h, ref in ((0, half0), (1, half1)):
                rows = slice(h * HALF, (h + 1) * HALF)
                y = ref[last, t, 0, 0].astype(F32)
                own[t, rows, :] = ((y - gap * v[rows]) * inverse).astype(BF)

        def correct(q, _):
            sub, y, z = place[0, q], place[1, q], place[2, q]
            gap = (alpha - local_stats[y, z, pl.ds(sub, 1), :]) * sigma
            top = local0[sub, y, z].astype(F32) - gap * picked[q, :HALF, :].astype(F32)
            picked[q, :HALF, :] = (top * inverse).astype(BF)
            low = local1[sub, z, y].astype(F32) - gap * picked[q, HALF:, :].astype(F32)
            picked[q, HALF:, :] = (low * inverse).astype(BF)
            return 0

        lax.fori_loop(0, BLK * ENT, correct, 0)

        one = jnp.ones((1, BD), F32)
        for t in range(BLK):
            combine(t)
            finish(p, t, contract(t, 0, CH), one, beta)

        @pl.when(k < APPS - 1)
        def _():
            for g in range(len(GROUPS)):
                gather_first(p, g)

        stats_first(p)
        stats_second(p)

        @pl.when(k < APPS - 1)
        def _():
            for g in range(len(GROUPS)):
                gather_second(p, g)

        return coefs, one

    coefs, _ = lax.fori_loop(1, APPS, application, (jnp.zeros((1, BD), F32), sigma0))

    p = APPS % 2
    stats_end(p)
    alpha, _ = scalars(p)
    coefs = jnp.where(lane == 2 * APPS - 2, alpha, coefs)
    out_coef[...] = coefs[:, :2 * APPS - 1]
    for t in range(BLK):
        out_vector[t] = own[t]
        gap = alpha - stats[p, 0, 0, 1, t:t + 1, :]
        out_rest[t] = leftover[t] - gap * own[t].astype(F32)

    def sent(step, _):
        b = step // CHUNKS
        c = step % CHUNKS

        @pl.when(seg < segs - 1)
        def _():
            env_copy(0, b, c).wait_send()

        @pl.when(seg > 0)
        def _():
            env_copy(1, b, c).wait_send()

        return 0

    lax.fori_loop(0, BLK * CHUNKS, sent, 0)


def on_device(segs, count, psi, env_left, env_right, site_left, site_right, mix_left, mix_right, sources, terms, term_coef, energy):
    vmem = pl.BlockSpec(memory_space=pltpu.VMEM)
    smem = pl.BlockSpec(memory_space=pltpu.SMEM)
    hbm = pl.BlockSpec(memory_space=pl.ANY)
    dma = pltpu.SemaphoreType.DMA
    groups = len(GROUPS)
    vector, rest, coefs = pl.pallas_call(
        functools.partial(kernel, segs, count),
        out_shape=(
            jax.ShapeDtypeStruct((BLK, BD, BD), BF),
            jax.ShapeDtypeStruct((BLK, BD, BD), F32),
            jax.ShapeDtypeStruct((1, 2 * APPS - 1), F32),
        ),
        in_specs=[vmem, hbm, hbm, vmem, vmem, vmem, vmem, smem, smem, vmem, vmem],
        out_specs=(vmem, vmem, vmem),
        scratch_shapes=[
            pltpu.VMEM((2, BLK, CH, BD, BD), BF),
            pltpu.VMEM((2, BLK, CH, BD, BD), BF),
            pltpu.VMEM((2, BLK, CH, BD, BD), BF),
            pltpu.VMEM((CHUNK, BD, BD), BF),
            pltpu.VMEM((2, 2, CH * TILE, CH * TILE), BF),
            pltpu.VMEM((2, BLK, BD, BD), BF),
            pltpu.VMEM((BLK, CH * TILE, 2 * ENT * TILE), BF),
            pltpu.VMEM((BLK, CH, BD, BD), BF),
            pltpu.VMEM((BLK, BD, BD), F32),
            pltpu.VMEM((BLK, BD, BD), F32),
            pltpu.VMEM((BLK * ENT, BD, BD), BF),
            pltpu.VMEM((BLK, BD, BD), BF),
            pltpu.VMEM((BLK, BD, BD), F32),
            pltpu.VMEM((BLK, BD, BD), F32),
            pltpu.VMEM((2, BLK, 4, 4, HALF, BD), BF),
            pltpu.VMEM((2, BLK, 4, 4, HALF, BD), BF),
            pltpu.VMEM((2, 4, 4, 2, 8, BD), F32),
            pltpu.VMEM((BLK, 4, 4, HALF, BD), BF),
            pltpu.VMEM((BLK, 4, 4, HALF, BD), BF),
            pltpu.VMEM((4, 4, 8, BD), F32),
            pltpu.SMEM((3, BLK * ENT), jnp.int32),
            dma((2, BLK + 1)),
            dma((2, BLK, CHUNKS)),
            dma((2, BLK, CHUNKS)),
            dma((2, groups, 2)),
            dma((2, groups, 2)),
            dma((2, groups, 2)),
            dma((2, groups, 2)),
            dma((2, 2)),
            dma((2, 2)),
        ],
        compiler_params=pltpu.CompilerParams(
            collective_id=0, has_side_effects=True, vmem_limit_bytes=56 * 2**20
        ),
        name="lanczos",
    )(
        psi[0], env_left[0], env_right[0], site_left[0], site_right[0], mix_left[0], mix_right[0],
        sources[0], terms[0], term_coef, energy[0],
    )
    return vector[None], rest[None], coefs


def solution(mesh):
    in_specs = (
        P("seg", "sec", None, None),
        P("seg", "sec", None, None, None),
        P("seg", "sec", None, None, None),
        P("seg", "sec", None, None),
        P("seg", "sec", None, None),
        P("seg", None, None),
        P("seg", None, None),
        P("seg", "sec", None),
        P("seg", "sec", None),
        P(),
        P("seg", "sec", None),
    )
    out_specs = (P("seg", "sec", None, None), P("seg", "sec", None, None), P("seg", None))
    segs = mesh.shape["seg"]
    count = float(BLK * mesh.shape["sec"] * BD * BD)
    return jax.shard_map(
        functools.partial(on_device, segs, count), mesh=mesh, in_specs=in_specs, out_specs=out_specs, check_vma=False
    )
```

time: 845 us -> 176 us (0.21)
  blocking collectives: 455 us -> 0 us
  waiting for transfers between devices: 209 us -> 0 us
  Pallas kernels: 0 us -> 169 us
  matrix products: 116 us -> 0 us
  between operations: 22.6 us -> 0.64 us
  other arithmetic: 15 us -> 0 us
    psum x12 -> x0, blocking collectives: 455 us -> none  [the longest x5 194 us: on_device(): alpha = lax.psum(jnp.sum(current_f * image), 'sec') / count]
    all_gather x6 -> x0, waiting for transfers between devices: 209 us -> none  [apply_operator(): piece = lax.all_gather(vector, 'sec', axis=0, tiled=True)]
    pallas_call x0 -> x1, Pallas kernels: none -> 169 us  [on_device(): pl.pallas_call(functools.partial(kernel, segs, count), out_shape=(jax.Sha...]
    dot_general x18 -> x0, matrix products: 116 us -> none  [the longest x6 45.4 us: apply_operator(): jnp.einsum('twik,twlk->til', inner, right_env, preferred_element_type=jnp...]
  transfers between devices with their start and end apart: 8 -> 0, of which waited for: 5 -> 0; matrix products, arithmetic and copies ran while one was open for 5% -> 0% of each run, Pallas kernels for 0% -> 0%
where the time goes in v1:
time: 176 us
  Pallas kernels  169 us (96%)
  local copies, waits for them, and re-layouts  6.82 us (4%)
    pallas_call x1, Pallas kernels, on_device(): pl.pallas_call(functools.partial(kernel, segs, count), out_shape=(jax.Sha...  169 us
    unnamed x5, local copies, waits for them, and re-layouts  6.82 us

profile of v1, /device:TPU:0, one launch (start us, length us, event | category | flops | bytes accessed | tf_op | source)
XLA Modules:
  0.0 176.2 jit_solution(18197576482449865331)
XLA Ops:
  0.6 1.3 copy.20
  1.9 1.3 copy_bitcast_fusion.1
  3.2 168.8 %lanczos.1 = (bf16[3,128,128]{2,1,0:T(8,128)(2,1)}, f32[3,128,128]{2,1,0:T(8,128)}, f32[1,11]{1,0:T(1,128)}) custom-call(bf16[3,128,128]{2,1,0:T(8,128)(2,1)} %bitcast.19, bf16[3,40,128,128]{3,2,1,0:T(8,128)(2,1)} %bitcast.16, bf16[3,40,128,128]{3,2,1,0:T(8,128)(2,1)} %bitcast.17, bf16[3,128,128]{2,1,0:T(8,128)(2,1)} %bitcast.20, ...), custom_call_target="tpu_custom_call" | custom-call | tf_op jit(solution)/shard_map/lanczos/pallas_call | solution.py:505
  171.9 1.5 copy.24
  173.5 1.6 copy.25
  175.1 1.1 copy.26

commit v2 on v1

--- a/solution.py
+++ b/solution.py
@@ -21,7 +21,8 @@
 
 CHUNK = 8
 CHUNKS = CH // CHUNK
-GROUPS = ((0, 3),)
+LANES = BD // 2
+PEERS = tuple((z, y) for z in range(4) for y in range(4) if (z, y) != (0, 0))
 
 
 def dot(a, b):
@@ -79,6 +80,8 @@
     envs,
     mixed,
     mix_kron,
+    pattern,
+    chooser,
     site_t,
     term_kron,
     combo,
@@ -116,6 +119,9 @@
     def along_y(d):
         return (seg, my_z * 4 + (my_y + d) % 4)
 
+    def along_both(dz, dy):
+        return (seg, ((my_z + dz) % 4) * 4 + (my_y + dy) % 4)
+
     def send(src, dst, ssem, rsem, device):
         pltpu.make_async_remote_copy(
             src_ref=src, dst_ref=dst, send_sem=ssem, recv_sem=rsem,
@@ -129,10 +135,12 @@
             c.start()
             loads.append(c)
 
+    for p in range(2):
+        stats[p, 0] = jnp.zeros((8, BD), F32)
+
     barrier = pltpu.get_barrier_semaphore()
-    for d in (1, 2, 3):
-        pl.semaphore_signal(barrier, inc=1, device_id=along_z(d), device_id_type=MESH)
-        pl.semaphore_signal(barrier, inc=1, device_id=along_y(d), device_id_type=MESH)
+    for dz, dy in PEERS:
+        pl.semaphore_signal(barrier, inc=1, device_id=along_both(dz, dy), device_id_type=MESH)
 
     @pl.when(seg > 0)
     def _():
@@ -154,17 +162,15 @@
     def _():
         end_copy(1).start()
 
-    for side, ref in ((0, mix_left), (1, mix_right)):
+    pattern[...] = jnp.where(same_state(BD, CH * TILE), 1.0, 0.0).astype(BF)
+    chooser[...] = spread(CH * TILE, 0)
+
+    def spread_mix(side, c, rows):
+        ref = mix_left if side == 0 else mix_right
+        chosen = chooser[rows, :]
         for part, mix in enumerate(split(ref[...])):
-            def build(m, _, side=side, part=part, mix=mix):
-                rows = dot(spread(BD, m * BD), mix).astype(BF)
-                full = dot_nt(rows, spread(CH * TILE, 0))
-                keep = same_state(BD, CH * TILE)
-                at = pl.ds(pl.multiple_of(m * BD, BD), BD)
-                mix_kron[side, part, at, :] = jnp.where(keep, full, 0.0).astype(BF)
-                return 0
-
-            lax.fori_loop(0, CH * TILE // BD, build, 0)
+            full = dot_nt(dot(chosen, mix).astype(BF), chooser[...])
+            mix_kron[side, part, rows, :] = full.astype(BF) * pattern[...]
 
     eye_row = lax.broadcasted_iota(jnp.int32, (BD, BD), 0)
     eye = (eye_row == lax.broadcasted_iota(jnp.int32, (BD, BD), 1)).astype(BF)
@@ -172,56 +178,46 @@
         for b in range(BLK):
             site_t[side, b] = dot_nt(eye, ref[b]).astype(BF)
 
-    for p in range(2):
-        stats[p, 0, 0] = jnp.zeros((2, 8, BD), F32)
     for t in range(BLK):
         half0[0, t, 0, 0] = psi[t, :HALF, :]
         half1[0, t, 0, 0] = psi[t, HALF:, :]
         own[t] = psi[t]
 
     pl.semaphore_wait(
-        barrier, 6 + jnp.where(seg > 0, 1, 0) + jnp.where(seg < segs - 1, 1, 0)
+        barrier, len(PEERS) + jnp.where(seg > 0, 1, 0) + jnp.where(seg < segs - 1, 1, 0)
     )
 
-    def gather_first(p, g):
-        ts = pl.ds(*GROUPS[g])
+    def gather_first(p, t):
         for d in (1, 3, 2):
             back = (4 - d) % 4
-            send(half0.at[p, ts, 0, 0], half0.at[p, ts, 0, back], s1.at[p, g, 0], r1.at[p, g, 0], along_z(d))
-            send(half1.at[p, ts, 0, 0], half1.at[p, ts, 0, back], s1.at[p, g, 1], r1.at[p, g, 1], along_y(d))
-
-    def gather_second(p, g):
-        ts = pl.ds(*GROUPS[g])
+            send(half0.at[p, t, 0, 0], half0.at[p, t, 0, back], s1.at[p, t, 0], r1.at[p, t, 0], along_z(d))
+            send(half1.at[p, t, 0, 0], half1.at[p, t, 0, back], s1.at[p, t, 1], r1.at[p, t, 1], along_y(d))
+
+    def gather_second(p, t):
         for h, ref, along in ((0, half0, along_y), (1, half1, along_z)):
-            wait_bytes(ref.at[p, ts, 0, pl.ds(1, 3)], r1.at[p, g, h])
+            wait_bytes(ref.at[p, t, 0, pl.ds(1, 3)], r1.at[p, t, h])
             for d in (1, 3, 2):
                 back = (4 - d) % 4
-                send(ref.at[p, ts, 0], ref.at[p, ts, back], s2.at[p, g, h], r2.at[p, g, h], along(d))
-
-    def gather_end(p):
-        for g, group in enumerate(GROUPS):
-            ts = pl.ds(*group)
-            for h, ref in ((0, half0), (1, half1)):
-                wait_bytes(ref.at[p, ts, pl.ds(1, 3)], r2.at[p, g, h])
-                wait_bytes(ref.at[p, ts, 0, pl.ds(1, 3)], s1.at[p, g, h])
-                wait_bytes(ref.at[p, ts, pl.ds(1, 3)], s2.at[p, g, h])
+                send(ref.at[p, t, 0], ref.at[p, t, back], s2.at[p, t, h], r2.at[p, t, h], along(d))
+
+    def gather_end(p, t):
+        for h, ref, local in ((0, half0, local0), (1, half1, local1)):
+            wait_bytes(ref.at[p, t, pl.ds(1, 3)], r2.at[p, t, h])
+            local[t] = ref[p, t]
+            wait_bytes(ref.at[p, t, 0, pl.ds(1, 3)], s1.at[p, t, h])
+            wait_bytes(ref.at[p, t, pl.ds(1, 3)], s2.at[p, t, h])
 
     def stats_first(p):
-        for d in (1, 3, 2):
-            send(stats.at[p, 0, 0], stats.at[p, 0, (4 - d) % 4], stat_send.at[p, 0], stat_recv.at[p, 0], along_z(d))
-
-    def stats_second(p):
-        wait_bytes(stats.at[p, 0, pl.ds(1, 3)], stat_recv.at[p, 0])
-        for d in (1, 3, 2):
-            send(stats.at[p, 0], stats.at[p, (4 - d) % 4], stat_send.at[p, 1], stat_recv.at[p, 1], along_y(d))
+        for dz, dy in PEERS:
+            back = (4 - dy) % 4 * 4 + (4 - dz) % 4
+            send(stats.at[p, 0], stats.at[p, back], stat_send.at[p], stat_recv.at[p], along_both(dz, dy))
 
     def stats_end(p):
-        wait_bytes(stats.at[p, pl.ds(1, 3)], stat_recv.at[p, 1])
-        wait_bytes(stats.at[p, 0, pl.ds(1, 3)], stat_send.at[p, 0])
-        wait_bytes(stats.at[p, pl.ds(1, 3)], stat_send.at[p, 1])
-
-    for g in range(len(GROUPS)):
-        gather_first(0, g)
+        wait_bytes(stats.at[p, pl.ds(1, 15)], stat_recv.at[p])
+        wait_bytes(stats.at[p, pl.ds(1, 15)], stat_send.at[p])
+
+    for t in range(BLK):
+        gather_first(0, t)
 
     def env_copy(side, b, c):
         part = pl.ds(c * CHUNK, CHUNK)
@@ -244,6 +240,11 @@
                 wait_bytes(env_in.at[side, b], load_sem.at[side, b])
 
             rows = pl.ds(pl.multiple_of(c * CHUNK * TILE, CHUNK * TILE), CHUNK * TILE)
+
+            @pl.when(b == 0)
+            def _(side=side, rows=rows):
+                spread_mix(side, c, rows)
+
             high = mix_kron[side, 0, rows, :]
             low = mix_kron[side, 1, rows, :]
             for i in range(BD // (2 * TILE)):
@@ -272,11 +273,11 @@
 
     lax.fori_loop(0, BLK * CHUNKS, grow, 0)
 
-    for g in range(len(GROUPS)):
-        gather_second(0, g)
-
-    for t in range(BLK):
-        row = jnp.broadcast_to(energy[t:t + 1, :], (BD, BD))
+    for t in range(BLK):
+        gather_second(0, t)
+
+    for t in range(BLK):
+        row = jnp.broadcast_to(energy[t], (BD, BD))
         on_site[t] = jnp.transpose(row)
     spread_all = spread(CH * TILE, 0)
     keep = same_state(CH * TILE, ENT * TILE)
@@ -284,7 +285,7 @@
         entry = lax.broadcasted_iota(jnp.int32, (8, ENT * TILE), 1) // TILE
         kind = jnp.zeros((8, ENT * TILE), jnp.int32)
         for k in range(ENT):
-            kind = jnp.where(entry == k, terms[t, k], kind)
+            kind = jnp.where(entry == k, terms[t, 0, k], kind)
         hit = (kind == lax.broadcasted_iota(jnp.int32, (8, ENT * TILE), 0)).astype(BF)
         for part, coef in enumerate(split(term_coef[...])):
             rows = dot_nt(spread_all, coef).astype(BF)
@@ -292,7 +293,7 @@
             term_kron[t, :, part * ENT * TILE:(part + 1) * ENT * TILE] = jnp.where(keep, full, 0.0).astype(BF)
 
     def where_is(t, k):
-        s = sources[t, k]
+        s = sources[t, 0, k]
         owner = s // BLK
         sub = s - BLK * owner
         return sub, (owner % 4 - my_y + 4) % 4, (owner // 4 - my_z + 4) % 4
@@ -302,10 +303,8 @@
             for n, value in enumerate(where_is(t, k)):
                 place[n, t * ENT + k] = value
 
-    gather_end(0)
-
-    local0[...] = half0[0]
-    local1[...] = half1[0]
+    for t in range(BLK):
+        gather_end(0, t)
 
     def fetch(q, _):
         sub, y, z = place[0, q], place[1, q], place[2, q]
@@ -318,13 +317,15 @@
     def squares(n, acc):
         t, o = n // 4, n % 4
         for i in range(4):
-            for ref in (half0, half1):
-                x = ref[0, t, o, i].astype(F32)
+            for ref in (local0, local1):
+                x = ref[t, o, i].astype(F32)
                 acc = acc + x * x
         return acc
 
     norm = total(lax.fori_loop(0, BLK * 4, squares, jnp.zeros((HALF, BD), F32)))
     sigma0 = 1.0 / jnp.sqrt(norm / count + EPSILON)
+
+    lane = lax.broadcasted_iota(jnp.int32, (1, BD), 1)
 
     def combine(t):
         for i in range(BD // (2 * TILE)):
@@ -358,19 +359,22 @@
         low = y.astype(BF)
         half0[p, t, 0, 0] = low[:HALF]
         half1[p, t, 0, 0] = low[HALF:]
-        stats[p, 0, 0, 0, t:t + 1, :] = prod
-        stats[p, 0, 0, 0, 4 + t:5 + t, :] = norm
-        stats[p, 0, 0, 1, t:t + 1, :] = a
-        stats[p, 0, 0, 1, 4 + t:5 + t, :] = total(y * y)
+        stats[p, 0, t:t + 1, :] = jnp.where(lane < LANES, prod, norm)
+        stats[p, 0, 4 + t:5 + t, :] = jnp.where(lane < LANES, a, total(y * y))
 
     def scalars(p):
         def add(x):
             lines = jnp.sum(x.reshape(16, 4, BD), axis=0)
             return jnp.sum(lines, axis=0, keepdims=True)
 
-        alpha = add(stats[p, :, :, 0, 0:4, :]) / count
-        gap = alpha - stats[p, :, :, 1, 0:4, :]
-        squared = stats[p, :, :, 1, 4:8, :] + gap * gap * stats[p, :, :, 0, 4:8, :]
+        got = stats[p]
+        turned = pltpu.roll(got.reshape(16 * 8, BD), LANES, 1).reshape(16, 8, BD)
+        first = jnp.where(lane < LANES, got, turned)
+        second = jnp.where(lane < LANES, turned, got)
+        local_stats[...] = first
+        alpha = add(first[:, 0:4, :]) / count
+        gap = alpha - first[:, 4:8, :]
+        squared = second[:, 4:8, :] + gap * gap * second[:, 0:4, :]
         return alpha, jnp.sqrt(add(squared) / count + EPSILON)
 
     for t in range(BLK):
@@ -386,32 +390,27 @@
 
     image[...] = jnp.zeros_like(image)
 
-    def apply_first(step, _):
-        b = step // CHUNKS
-        c = step % CHUNKS
-
-        @pl.when(seg > 0)
-        def _():
-            env_copy(0, b, c).wait_recv()
-
-        @pl.when(seg < segs - 1)
-        def _():
-            env_copy(1, b, c).wait_recv()
-
-        image[b] = image[b] + contract(b, c * CHUNK, CHUNK)
-        return 0
-
-    lax.fori_loop(0, BLK * CHUNKS, apply_first, 0)
-    for t in range(BLK):
-        finish(1, t, image[t], sigma0, None)
-    for g in range(len(GROUPS)):
-        gather_first(1, g)
-    stats_first(1)
-    stats_second(1)
-    for g in range(len(GROUPS)):
-        gather_second(1, g)
-
-    lane = lax.broadcasted_iota(jnp.int32, (1, BD), 1)
+    for b in range(BLK):
+        def apply_first(c, _, b=b):
+            @pl.when(seg > 0)
+            def _():
+                env_copy(0, b, c).wait_recv()
+
+            @pl.when(seg < segs - 1)
+            def _():
+                env_copy(1, b, c).wait_recv()
+
+            image[b] = image[b] + contract(b, c * CHUNK, CHUNK)
+            return 0
+
+        lax.fori_loop(0, CHUNKS, apply_first, 0)
+        finish(1, b, image[b], sigma0, None)
+        if b == BLK - 1:
+            stats_first(1)
+        gather_first(1, b)
+        if b > 0:
+            gather_second(1, b - 1)
+    gather_second(1, BLK - 1)
 
     def application(k, carry):
         coefs, sigma = carry
@@ -422,23 +421,21 @@
         coefs = jnp.where(lane == 2 * k - 2, alpha, coefs)
         coefs = jnp.where(lane == 2 * k - 1, beta, coefs)
         inverse = 1.0 / beta
-        local_stats[...] = stats[last, :, :, 1]
-        gather_end(last)
-        local0[...] = half0[last]
-        local1[...] = half1[last]
-
         for t in range(BLK):
-            gap = (alpha - stats[last, 0, 0, 1, t:t + 1, :]) * sigma
+            gather_end(last, t)
+
+        for t in range(BLK):
+            gap = (alpha - local_stats[0, 4 + t:5 + t, :]) * sigma
             v = own[t].astype(F32)
             before[t] = v * sigma
-            for h, ref in ((0, half0), (1, half1)):
+            for h, ref in ((0, local0), (1, local1)):
                 rows = slice(h * HALF, (h + 1) * HALF)
-                y = ref[last, t, 0, 0].astype(F32)
+                y = ref[t, 0, 0].astype(F32)
                 own[t, rows, :] = ((y - gap * v[rows]) * inverse).astype(BF)
 
         def correct(q, _):
             sub, y, z = place[0, q], place[1, q], place[2, q]
-            gap = (alpha - local_stats[y, z, pl.ds(sub, 1), :]) * sigma
+            gap = (alpha - local_stats[y * 4 + z, pl.ds(4 + sub, 1), :]) * sigma
             top = local0[sub, y, z].astype(F32) - gap * picked[q, :HALF, :].astype(F32)
             picked[q, :HALF, :] = (top * inverse).astype(BF)
             low = local1[sub, z, y].astype(F32) - gap * picked[q, HALF:, :].astype(F32)
@@ -451,19 +448,16 @@
         for t in range(BLK):
             combine(t)
             finish(p, t, contract(t, 0, CH), one, beta)
-
-        @pl.when(k < APPS - 1)
-        def _():
-            for g in range(len(GROUPS)):
-                gather_first(p, g)
-
-        stats_first(p)
-        stats_second(p)
-
-        @pl.when(k < APPS - 1)
-        def _():
-            for g in range(len(GROUPS)):
-                gather_second(p, g)
+            if t == BLK - 1:
+                stats_first(p)
+
+            @pl.when(k < APPS - 1)
+            def _(t=t):
+                gather_first(p, t)
+                if t > 0:
+                    gather_second(p, t - 1)
+                if t == BLK - 1:
+                    gather_second(p, t)
 
         return coefs, one
 
@@ -476,7 +470,7 @@
     out_coef[...] = coefs[:, :2 * APPS - 1]
     for t in range(BLK):
         out_vector[t] = own[t]
-        gap = alpha - stats[p, 0, 0, 1, t:t + 1, :]
+        gap = alpha - local_stats[0, 4 + t:5 + t, :]
         out_rest[t] = leftover[t] - gap * own[t].astype(F32)
 
     def sent(step, _):
@@ -494,6 +488,22 @@
         return 0
 
     lax.fori_loop(0, BLK * CHUNKS, sent, 0)
+
+
+def move(*refs):
+    for i in range(3):
+        refs[3 + i][...] = refs[i][...]
+
+
+def hand_on(*arrays):
+    hbm = pl.BlockSpec(memory_space=pltpu.VMEM)
+    return pl.pallas_call(
+        move,
+        out_shape=tuple(jax.ShapeDtypeStruct(a.shape, a.dtype) for a in arrays),
+        in_specs=[hbm] * 3,
+        out_specs=(hbm,) * 3,
+        name="hand_on",
+    )(*arrays)
 
 
 def on_device(segs, count, psi, env_left, env_right, site_left, site_right, mix_left, mix_right, sources, terms, term_coef, energy):
@@ -501,7 +511,6 @@
     smem = pl.BlockSpec(memory_space=pltpu.SMEM)
     hbm = pl.BlockSpec(memory_space=pl.ANY)
     dma = pltpu.SemaphoreType.DMA
-    groups = len(GROUPS)
     vector, rest, coefs = pl.pallas_call(
         functools.partial(kernel, segs, count),
         out_shape=(
@@ -517,6 +526,8 @@
             pltpu.VMEM((2, BLK, CH, BD, BD), BF),
             pltpu.VMEM((CHUNK, BD, BD), BF),
             pltpu.VMEM((2, 2, CH * TILE, CH * TILE), BF),
+            pltpu.VMEM((BD, CH * TILE), BF),
+            pltpu.VMEM((CH * TILE, CH), BF),
             pltpu.VMEM((2, BLK, BD, BD), BF),
             pltpu.VMEM((BLK, CH * TILE, 2 * ENT * TILE), BF),
             pltpu.VMEM((BLK, CH, BD, BD), BF),
@@ -528,20 +539,20 @@
             pltpu.VMEM((BLK, BD, BD), F32),
             pltpu.VMEM((2, BLK, 4, 4, HALF, BD), BF),
             pltpu.VMEM((2, BLK, 4, 4, HALF, BD), BF),
-            pltpu.VMEM((2, 4, 4, 2, 8, BD), F32),
+            pltpu.VMEM((2, 16, 8, BD), F32),
             pltpu.VMEM((BLK, 4, 4, HALF, BD), BF),
             pltpu.VMEM((BLK, 4, 4, HALF, BD), BF),
-            pltpu.VMEM((4, 4, 8, BD), F32),
+            pltpu.VMEM((16, 8, BD), F32),
             pltpu.SMEM((3, BLK * ENT), jnp.int32),
             dma((2, BLK + 1)),
             dma((2, BLK, CHUNKS)),
             dma((2, BLK, CHUNKS)),
-            dma((2, groups, 2)),
-            dma((2, groups, 2)),
-            dma((2, groups, 2)),
-            dma((2, groups, 2)),
-            dma((2, 2)),
-            dma((2, 2)),
+            dma((2, BLK, 2)),
+            dma((2, BLK, 2)),
+            dma((2, BLK, 2)),
+            dma((2, BLK, 2)),
+            dma((2,)),
+            dma((2,)),
         ],
         compiler_params=pltpu.CompilerParams(
             collective_id=0, has_side_effects=True, vmem_limit_bytes=56 * 2**20
@@ -549,8 +560,9 @@
         name="lanczos",
     )(
         psi[0], env_left[0], env_right[0], site_left[0], site_right[0], mix_left[0], mix_right[0],
-        sources[0], terms[0], term_coef, energy[0],
+        jnp.transpose(sources, (1, 0, 2)), jnp.transpose(terms, (1, 0, 2)), term_coef, jnp.transpose(energy, (1, 0, 2)),
     )
+    vector, rest, coefs = hand_on(vector, rest, coefs)
     return vector[None], rest[None], coefs
 
 

time: 176 us -> 159 us (0.903)
  Pallas kernels: 169 us -> 158 us
  local copies, waits for them, and re-layouts: 6.82 us -> 0 us
    pallas_call x1, Pallas kernels: 169 us -> 156 us  [on_device(): pl.pallas_call(functools.partial(kernel, segs, count), out_shape=(jax.Sha...]
    unnamed x5 -> x0, local copies, waits for them, and re-layouts: 6.82 us -> none
where the time goes in v2:
time: 159 us
  Pallas kernels  158 us (99%)
    pallas_call x1, Pallas kernels, on_device(): pl.pallas_call(functools.partial(kernel, segs, count), out_shape=(jax.Sha...  156 us

profile of v2, /device:TPU:0, one launch (start us, length us, event | category | flops | bytes accessed | tf_op | source)
XLA Modules:
  0.0 158.8 jit_solution(4861662942094468332)
XLA Ops:
  0.6 156.5 %lanczos.1 = (bf16[3,128,128]{2,1,0:T(8,128)(2,1)}, f32[3,128,128]{2,1,0:T(8,128)}, f32[1,11]{1,0:T(1,128)}) custom-call(bf16[3,128,128]{2,1,0:T(8,128)(2,1)} %bitcast.14, bf16[3,40,128,128]{3,2,1,0:T(8,128)(2,1)} %bitcast.12, bf16[3,40,128,128]{3,2,1,0:T(8,128)(2,1)} %bitcast.13, bf16[3,128,128]{2,1,0:T(8,128)(2,1)} %bitcast.15, ...), custom_call_target="tpu_custom_call" | custom-call | tf_op jit(solution)/shard_map/lanczos/pallas_call | solution.py:514
  157.1 1.7 %hand_on.1 = (bf16[3,128,128]{2,1,0:T(8,128)(2,1)}, f32[3,128,128]{2,1,0:T(8,128)}, f32[1,11]{1,0:T(1,128)}) custom-call(bf16[3,128,128]{2,1,0:T(8,128)(2,1)} %get-tuple-element.9.refs_0_, f32[3,128,128]{2,1,0:T(8,128)} %get-tuple-element.10.refs_1_, f32[1,11]{1,0:T(1,128)} %get-tuple-element.11.refs_2_), custom_call_target="tpu_custom_call" | custom-call | tf_op jit(solution)/shard_map/hand_on/pallas_call | solution.py:500

commit v3 on v2

v3 whole, which is shorter than its diff:
```python
import functools

import jax
import jax.numpy as jnp
from jax import lax
from jax.experimental import pallas as pl
from jax.experimental.pallas import tpu as pltpu
from jax.sharding import PartitionSpec as P

APPS = 6
EPSILON = 1e-06
CH = 40
BD = 128
ENT = 6
BLK = 3
HALF = BD // 2
TILE = 16
BY_ID = pl.DeviceIdType.LOGICAL
BF = jnp.bfloat16
F32 = jnp.float32

CHUNK = 8
CHUNKS = CH // CHUNK
LANES = BD // 2
ROWS = BD + TILE
PEERS = tuple((z, y) for z in range(4) for y in range(4) if (z, y) != (0, 0))


def dot(a, b):
    return lax.dot_general(a, b, (((1,), (0,)), ((), ())), preferred_element_type=F32)


def dot_nt(a, b):
    return lax.dot_general(a, b, (((1,), (1,)), ((), ())), preferred_element_type=F32)


def total(x):
    lanes = jnp.sum(x, axis=0, keepdims=True)
    return jnp.broadcast_to(jnp.sum(lanes, axis=1, keepdims=True), (1, BD))


def split(x):
    high = x.astype(BF)
    return high, (x - high.astype(F32)).astype(BF)


def wait_bytes(ref, sem):
    pltpu.make_async_copy(ref, ref, sem).wait()


def spread(rows, start):
    row = lax.broadcasted_iota(jnp.int32, (rows, CH), 0) + start
    return (row // TILE == lax.broadcasted_iota(jnp.int32, (rows, CH), 1)).astype(BF)


def same_state(rows, cols):
    row = lax.broadcasted_iota(jnp.int32, (rows, cols), 0)
    col = lax.broadcasted_iota(jnp.int32, (rows, cols), 1)
    return row % TILE == col % TILE


def kernel(
    segs,
    count,
    psi,
    env_left,
    env_right,
    site_left,
    site_right,
    mix_left,
    mix_right,
    sources,
    terms,
    term_coef,
    energy,
    out_vector,
    out_rest,
    out_coef,
    env_in,
    grown,
    envs,
    mixed,
    mix_kron,
    mix_parts,
    sites,
    pattern,
    chooser,
    site_t,
    term_kron,
    combo,
    image,
    on_site,
    picked,
    own,
    before,
    leftover,
    pieces,
    stats,
    local,
    facts,
    place,
    load_sem,
    env_send,
    env_recv,
    ssem,
    rsem,
    stat_send,
    stat_recv,
):
    seg = lax.axis_index("seg")
    sec = lax.axis_index("sec")
    my_z = sec // 4
    my_y = sec % 4

    def at(z, y):
        return seg * 16 + z * 4 + y

    to_z = {d: at((my_z + d) % 4, my_y) for d in (1, 2, 3)}
    to_y = {d: at(my_z, (my_y + d) % 4) for d in (1, 2, 3)}
    to_peer = {(dz, dy): at((my_z + dz) % 4, (my_y + dy) % 4) for dz, dy in PEERS}
    here = at(my_z, my_y)

    def send(src, dst, ssem, rsem, device):
        pltpu.make_async_remote_copy(
            src_ref=src, dst_ref=dst, send_sem=ssem, recv_sem=rsem,
            device_id=device, device_id_type=BY_ID,
        ).start()

    loads = []
    for b in range(BLK):
        for side, ref in ((0, env_left), (1, env_right)):
            c = pltpu.make_async_copy(ref.at[b], env_in.at[side, b], load_sem.at[side, b])
            c.start()
            loads.append(c)

    stats[0] = jnp.zeros((8, BD), F32)

    barrier = pltpu.get_barrier_semaphore()
    for dz, dy in PEERS:
        pl.semaphore_signal(barrier, inc=1, device_id=to_peer[dz, dy], device_id_type=BY_ID)

    @pl.when(seg > 0)
    def _():
        pl.semaphore_signal(barrier, inc=1, device_id=here - 16, device_id_type=BY_ID)

    @pl.when(seg < segs - 1)
    def _():
        pl.semaphore_signal(barrier, inc=1, device_id=here + 16, device_id_type=BY_ID)

    def end_copy(side):
        source = env_left if side == 0 else env_right
        return pltpu.make_async_copy(source, envs.at[side], load_sem.at[side, BLK])

    @pl.when(seg == 0)
    def _():
        end_copy(0).start()

    @pl.when(seg == segs - 1)
    def _():
        end_copy(1).start()

    pattern[...] = jnp.where(same_state(BD, CH * TILE), 1.0, 0.0).astype(BF)
    chooser[...] = spread(CH * TILE, 0)

    for side, (mix, site) in enumerate(((mix_left, site_left), (mix_right, site_right))):
        for part, value in enumerate(split(mix[...])):
            mix_parts[side, part] = value
        sites[side] = site[...]

    def spread_mix(side, rows):
        chosen = chooser[rows, :]
        for part in range(2):
            full = dot_nt(dot(chosen, mix_parts[side, part]).astype(BF), chooser[...])
            at = slice(part * CH * TILE, (part + 1) * CH * TILE)
            mix_kron[side, rows, at] = full.astype(BF) * pattern[...]

    eye_row = lax.broadcasted_iota(jnp.int32, (BD, BD), 0)
    eye = (eye_row == lax.broadcasted_iota(jnp.int32, (BD, BD), 1)).astype(BF)
    for side, ref in ((0, site_left), (1, site_right)):
        for b in range(BLK):
            site_t[side, b] = dot_nt(eye, ref[b]).astype(BF)

    for t in range(BLK):
        pieces[0, t, 0, 0, :BD, :] = psi[t]
        pieces[0, t, 0, 0, BD:, :] = jnp.zeros((TILE, BD), BF)
        own[t] = psi[t]

    pl.semaphore_wait(
        barrier, len(PEERS) + jnp.where(seg > 0, 1, 0) + jnp.where(seg < segs - 1, 1, 0)
    )

    axes = ((0, to_y, pl.ds(0, HALF)), (1, to_z, pl.ds(HALF, ROWS - HALF)))

    def direct(p, t, h):
        return pieces.at[p, t, 0, pl.ds(1, 3)] if h == 0 else pieces.at[p, t, pl.ds(1, 3), 0]

    def bundle(p, t, h, o, rows):
        return pieces.at[p, t, o, pl.ds(1, 3), rows] if h == 0 else pieces.at[p, t, pl.ds(1, 3), o, rows]

    def gather_first(p, t):
        mine = pieces.at[p, t, 0, 0]
        for d in (1, 3, 2):
            back = (4 - d) % 4
            send(mine, pieces.at[p, t, 0, back], ssem.at[p, t, 0, 0], rsem.at[p, t, 0, 0], to_z[d])
            send(mine, pieces.at[p, t, back, 0], ssem.at[p, t, 1, 0], rsem.at[p, t, 1, 0], to_y[d])

    def gather_second(p, t):
        for h, to, rows in axes:
            wait_bytes(direct(p, t, h), rsem.at[p, t, h, 0])
            for d in (1, 3, 2):
                back = (4 - d) % 4
                send(bundle(p, t, h, 0, rows), bundle(p, t, h, back, rows), ssem.at[p, t, h, 1], rsem.at[p, t, h, 1], to[d])

    def gather_end(p, t):
        for h, _, rows in axes:
            wait_bytes(pieces.at[p, t, pl.ds(1, 3), pl.ds(1, 3), rows], rsem.at[p, t, h, 1])
        local[t] = pieces[p, t]

    def gather_sent(p, t):
        for h, _, rows in axes:
            wait_bytes(direct(p, t, h), ssem.at[p, t, h, 0])
            wait_bytes(pieces.at[p, t, pl.ds(1, 3), pl.ds(1, 3), rows], ssem.at[p, t, h, 1])

    def gather_onward(p, t):
        if t > 0:
            gather_second(p, t - 1)
        if t == BLK - 1:
            gather_second(p, t)

    def stats_send():
        for dz, dy in PEERS:
            back = (4 - dy) % 4 * 4 + (4 - dz) % 4
            send(stats.at[0], stats.at[back], stat_send, stat_recv, to_peer[dz, dy])

    def stats_end():
        wait_bytes(stats.at[pl.ds(1, 15)], stat_recv)
        wait_bytes(stats.at[pl.ds(1, 15)], stat_send)

    def env_copy(side, b, c):
        part = pl.ds(c * CHUNK, CHUNK)
        to = here + 16 - 32 * side
        return pltpu.make_async_remote_copy(
            src_ref=grown.at[side, b, part],
            dst_ref=envs.at[side, b, part],
            send_sem=env_send.at[side, b, c],
            recv_sem=env_recv.at[side, b, c],
            device_id=to,
            device_id_type=BY_ID,
        )

    def grow(step, _):
        side = (step + 1 + seg) % 2
        b = step // 2 // CHUNKS
        c = step // 2 % CHUNKS
        rows = pl.ds(pl.multiple_of(c * CHUNK * TILE, CHUNK * TILE), CHUNK * TILE)

        @pl.when(c == 0)
        def _():
            wait_bytes(env_in.at[side, b], load_sem.at[side, b])

        @pl.when(b == 0)
        def _():
            spread_mix(side, rows)

        maps = mix_kron[side, rows, :]
        for i in range(BD // (2 * TILE)):
            base = i * 2 * TILE
            cols = [
                env_in[side, b, :, base + h * TILE:base + (h + 1) * TILE, :].reshape(CH * TILE, BD)
                for h in range(2)
            ]
            both = jnp.concatenate(cols, axis=1)
            out = dot(maps, jnp.concatenate([both, both], axis=0)).astype(BF)
            for h in range(2):
                mixed[:, base + h * TILE:base + (h + 1) * TILE, :] = out[:, h * BD:(h + 1) * BD].reshape(
                    CHUNK, TILE, BD
                )
        half = dot(mixed[...].reshape(CHUNK * BD, BD), sites[side, b]).astype(BF)
        wide = jnp.concatenate([half[v * BD:(v + 1) * BD] for v in range(CHUNK)], axis=1)
        done = dot(site_t[side, b], wide).astype(BF)
        for v in range(CHUNK):
            grown[side, b, c * CHUNK + v] = done[:, v * BD:(v + 1) * BD]

        @pl.when(jnp.where(side == 0, seg < segs - 1, seg > 0))
        def _():
            env_copy(side, b, c).start()

        return 0

    lax.fori_loop(0, 2 * CHUNKS, grow, 0)
    for t in range(BLK):
        gather_first(0, t)
    lax.fori_loop(2 * CHUNKS, 4 * CHUNKS, grow, 0)
    for t in range(BLK):
        gather_second(0, t)
    lax.fori_loop(4 * CHUNKS, 6 * CHUNKS, grow, 0)

    for t in range(BLK):
        row = jnp.broadcast_to(energy[t], (BD, BD))
        on_site[t] = jnp.transpose(row)
    spread_all = spread(CH * TILE, 0)
    keep = same_state(CH * TILE, ENT * TILE)
    for t in range(BLK):
        entry = lax.broadcasted_iota(jnp.int32, (8, ENT * TILE), 1) // TILE
        kind = jnp.zeros((8, ENT * TILE), jnp.int32)
        for k in range(ENT):
            kind = jnp.where(entry == k, terms[t, 0, k], kind)
        hit = (kind == lax.broadcasted_iota(jnp.int32, (8, ENT * TILE), 0)).astype(BF)
        for part, coef in enumerate(split(term_coef[...])):
            rows = dot_nt(spread_all, coef).astype(BF)
            full = dot(rows, hit)
            term_kron[t, :, part * ENT * TILE:(part + 1) * ENT * TILE] = jnp.where(keep, full, 0.0).astype(BF)

    def where_is(t, k):
        s = sources[t, 0, k]
        owner = s // BLK
        sub = s - BLK * owner
        return sub, (owner % 4 - my_y + 4) % 4, (owner // 4 - my_z + 4) % 4

    for t in range(BLK):
        for k in range(ENT):
            for n, value in enumerate(where_is(t, k)):
                place[n, t * ENT + k] = value

    for t in range(BLK):
        gather_end(0, t)
        gather_sent(0, t)

    def fetch(q, _):
        sub, y, z = place[0, q], place[1, q], place[2, q]
        picked[q] = local[sub, y, z, :BD, :]
        return 0

    lax.fori_loop(0, BLK * ENT, fetch, 0)

    def squares(n, acc):
        t, o = n // 4, n % 4
        for i in range(4):
            x = local[t, o, i, :BD, :].astype(F32)
            acc = acc + x * x
        return acc

    norm = total(lax.fori_loop(0, BLK * 4, squares, jnp.zeros((BD, BD), F32)))
    sigma0 = 1.0 / jnp.sqrt(norm / count + EPSILON)

    lane = lax.broadcasted_iota(jnp.int32, (1, BD), 1)

    def combine(t):
        for i in range(BD // (2 * TILE)):
            base = i * 2 * TILE
            cols = [
                picked[t * ENT:(t + 1) * ENT, base + h * TILE:base + (h + 1) * TILE, :].reshape(ENT * TILE, BD)
                for h in range(2)
            ]
            both = jnp.concatenate(cols, axis=1)
            out = dot(term_kron[t], jnp.concatenate([both, both], axis=0)).astype(BF)
            for h in range(2):
                combo[t, :, base + h * TILE:base + (h + 1) * TILE, :] = out[:, h * BD:(h + 1) * BD].reshape(
                    CH, TILE, BD
                )

    def contract(t, first, n):
        inner = [dot(envs[0, t, first + j], combo[t, first + j]).astype(BF) for j in range(n)]
        right = [envs[1, t, first + j] for j in range(n)]
        return dot_nt(jnp.concatenate(inner, axis=1), jnp.concatenate(right, axis=1))

    def finish(p, t, applied, sigma, beta, final=False):
        v = own[t].astype(F32) * sigma
        img = applied * sigma + on_site[t] * v
        w = img if beta is None else img - beta * before[t]
        prod = total(img * v)
        norm = total(v * v)
        over = total(w * v)
        a = jnp.where(norm > 0.0, over / jnp.where(norm > 0.0, norm, 1.0), 0.0)
        y = w - a * v
        if final:
            leftover[t] = w
            stats[0, t:t + 1, :] = prod
            return
        pieces[p, t, 0, 0, :BD, :] = y.astype(BF)
        row = lax.broadcasted_iota(jnp.int32, (TILE, BD), 0)
        kind = row % 4
        value = jnp.where(kind == 0, prod, jnp.where(kind == 1, norm, jnp.where(kind == 2, a, total(y * y))))
        one = value.astype(BF).astype(F32)
        two = (value - one).astype(BF).astype(F32)
        three = (value - one - two).astype(BF).astype(F32)
        tile = jnp.where(row < 4, one, jnp.where(row < 8, two, jnp.where(row < 12, three, 0.0)))
        pieces[p, t, 0, 0, BD:, :] = tile.astype(BF)

    def learn(t):
        parts = local[t, :, :, BD:, :].astype(F32).reshape(16, TILE, BD)
        facts[t] = parts[:, 0:4, :] + parts[:, 4:8, :] + parts[:, 8:12, :]

    def scalars():
        alpha = jnp.zeros((1, BD), F32)
        for t in range(BLK):
            alpha = alpha + jnp.sum(facts[t], axis=0)[0:1, :]
        alpha = alpha / count
        squared = jnp.zeros((1, BD), F32)
        for t in range(BLK):
            gap = alpha - facts[t, :, 2, :]
            new = facts[t, :, 3, :] + gap * gap * facts[t, :, 1, :]
            squared = squared + jnp.sum(new, axis=0, keepdims=True)
        return alpha, jnp.sqrt(squared / count + EPSILON)

    for t in range(BLK):
        combine(t)

    @pl.when(seg == 0)
    def _():
        end_copy(0).wait()

    @pl.when(seg == segs - 1)
    def _():
        end_copy(1).wait()

    image[...] = jnp.zeros_like(image)

    for b in range(BLK):
        def apply_first(c, _, b=b):
            @pl.when(seg > 0)
            def _():
                env_copy(0, b, c).wait_recv()

            @pl.when(seg < segs - 1)
            def _():
                env_copy(1, b, c).wait_recv()

            image[b] = image[b] + contract(b, c * CHUNK, CHUNK)
            return 0

        lax.fori_loop(0, CHUNKS, apply_first, 0)
        finish(1, b, image[b], sigma0, None)
        gather_first(1, b)
        gather_onward(1, b)

    def application(k, coefs, sigma, final):
        last = k % 2
        p = (k + 1) % 2
        for t in range(BLK):
            gather_end(last, t)
            learn(t)
        alpha, beta = scalars()
        coefs = jnp.where(lane == 2 * k - 2, alpha, coefs)
        coefs = jnp.where(lane == 2 * k - 1, beta, coefs)
        inverse = 1.0 / beta

        def correct(q, _):
            sub, y, z = place[0, q], place[1, q], place[2, q]
            gap = (alpha - facts[sub, y * 4 + z, 2:3, :]) * sigma
            new = local[sub, y, z, :BD, :].astype(F32) - gap * picked[q].astype(F32)
            picked[q] = (new * inverse).astype(BF)
            return 0

        one = jnp.ones((1, BD), F32)
        for t in range(BLK):
            lax.fori_loop(t * ENT, (t + 1) * ENT, correct, 0, unroll=True)
            gap = (alpha - facts[t, 0, 2:3, :]) * sigma
            v = own[t].astype(F32)
            before[t] = v * sigma
            own[t] = ((local[t, 0, 0, :BD, :].astype(F32) - gap * v) * inverse).astype(BF)
            combine(t)
            finish(p, t, contract(t, 0, CH), one, beta, final)
            if t == 0:
                for u in range(BLK):
                    gather_sent(last, u)
            if not final:
                gather_first(p, t)
                gather_onward(p, t)
        return coefs

    def step(k, carry):
        return application(k, carry[0], carry[1], False), jnp.ones((1, BD), F32)

    coefs, sigma = lax.fori_loop(1, APPS - 1, step, (jnp.zeros((1, BD), F32), sigma0))
    coefs = application(APPS - 1, coefs, sigma, True)
    stats_send()
    stats_end()
    alpha = jnp.sum(jnp.sum(stats[...], axis=0), axis=0, keepdims=True) / count
    out_coef[...] = jnp.where(lane == 2 * APPS - 2, alpha, coefs)[:, :2 * APPS - 1]
    for t in range(BLK):
        out_vector[t] = own[t]
        out_rest[t] = leftover[t] - alpha * own[t].astype(F32)

    def sent(step, _):
        b = step // CHUNKS
        c = step % CHUNKS

        @pl.when(seg < segs - 1)
        def _():
            env_copy(0, b, c).wait_send()

        @pl.when(seg > 0)
        def _():
            env_copy(1, b, c).wait_send()

        return 0

    lax.fori_loop(0, BLK * CHUNKS, sent, 0)


def move(*refs):
    for i in range(3):
        refs[3 + i][...] = refs[i][...]


def hand_on(*arrays):
    hbm = pl.BlockSpec(memory_space=pltpu.VMEM)
    return pl.pallas_call(
        move,
        out_shape=tuple(jax.ShapeDtypeStruct(a.shape, a.dtype) for a in arrays),
        in_specs=[hbm] * 3,
        out_specs=(hbm,) * 3,
        name="hand_on",
    )(*arrays)


def on_device(segs, count, psi, env_left, env_right, site_left, site_right, mix_left, mix_right, sources, terms, term_coef, energy):
    vmem = pl.BlockSpec(memory_space=pltpu.VMEM)
    smem = pl.BlockSpec(memory_space=pltpu.SMEM)
    hbm = pl.BlockSpec(memory_space=pl.ANY)
    dma = pltpu.SemaphoreType.DMA
    vector, rest, coefs = pl.pallas_call(
        functools.partial(kernel, segs, count),
        out_shape=(
            jax.ShapeDtypeStruct((BLK, BD, BD), BF),
            jax.ShapeDtypeStruct((BLK, BD, BD), F32),
            jax.ShapeDtypeStruct((1, 2 * APPS - 1), F32),
        ),
        in_specs=[vmem, hbm, hbm, vmem, vmem, vmem, vmem, smem, smem, vmem, vmem],
        out_specs=(vmem, vmem, vmem),
        scratch_shapes=[
            pltpu.VMEM((2, BLK, CH, BD, BD), BF),
            pltpu.VMEM((2, BLK, CH, BD, BD), BF),
            pltpu.VMEM((2, BLK, CH, BD, BD), BF),
            pltpu.VMEM((CHUNK, BD, BD), BF),
            pltpu.VMEM((2, CH * TILE, 2 * CH * TILE), BF),
            pltpu.VMEM((2, 2, CH, CH), BF),
            pltpu.VMEM((2, BLK, BD, BD), BF),
            pltpu.VMEM((BD, CH * TILE), BF),
            pltpu.VMEM((CH * TILE, CH), BF),
            pltpu.VMEM((2, BLK, BD, BD), BF),
            pltpu.VMEM((BLK, CH * TILE, 2 * ENT * TILE), BF),
            pltpu.VMEM((BLK, CH, BD, BD), BF),
            pltpu.VMEM((BLK, BD, BD), F32),
            pltpu.VMEM((BLK, BD, BD), F32),
            pltpu.VMEM((BLK * ENT, BD, BD), BF),
            pltpu.VMEM((BLK, BD, BD), BF),
            pltpu.VMEM((BLK, BD, BD), F32),
            pltpu.VMEM((BLK, BD, BD), F32),
            pltpu.VMEM((2, BLK, 4, 4, ROWS, BD), BF),
            pltpu.VMEM((16, 8, BD), F32),
            pltpu.VMEM((BLK, 4, 4, ROWS, BD), BF),
            pltpu.VMEM((BLK, 16, 4, BD), F32),
            pltpu.SMEM((3, BLK * ENT), jnp.int32),
            dma((2, BLK + 1)),
            dma((2, BLK, CHUNKS)),
            dma((2, BLK, CHUNKS)),
            dma((2, BLK, 2, 2)),
            dma((2, BLK, 2, 2)),
            dma,
            dma,
        ],
        compiler_params=pltpu.CompilerParams(
            collective_id=0, has_side_effects=True, vmem_limit_bytes=56 * 2**20
        ),
        name="lanczos",
    )(
        psi[0], env_left[0], env_right[0], site_left[0], site_right[0], mix_left[0], mix_right[0],
        jnp.transpose(sources, (1, 0, 2)), jnp.transpose(terms, (1, 0, 2)), term_coef, jnp.transpose(energy, (1, 0, 2)),
    )
    vector, rest, coefs = hand_on(vector, rest, coefs)
    return vector[None], rest[None], coefs


def solution(mesh):
    in_specs = (
        P("seg", "sec", None, None),
        P("seg", "sec", None, None, None),
        P("seg", "sec", None, None, None),
        P("seg", "sec", None, None),
        P("seg", "sec", None, None),
        P("seg", None, None),
        P("seg", None, None),
        P("seg", "sec", None),
        P("seg", "sec", None),
        P(),
        P("seg", "sec", None),
    )
    out_specs = (P("seg", "sec", None, None), P("seg", "sec", None, None), P("seg", None))
    segs = mesh.shape["seg"]
    count = float(BLK * mesh.shape["sec"] * BD * BD)
    return jax.shard_map(
        functools.partial(on_device, segs, count), mesh=mesh, in_specs=in_specs, out_specs=out_specs, check_vma=False
    )
```

time: 159 us -> 152 us (0.956); the launches traced: 159 us -> 150 us
  Pallas kernels: 158 us -> 149 us
    pallas_call x1, Pallas kernels: 156 us -> 148 us  [on_device(): pl.pallas_call(functools.partial(kernel, segs, count), out_shape=(jax.Sha...]
where the time goes in v3:
time: 152 us; the launch traced here: 150 us
  Pallas kernels  149 us (98%)
    pallas_call x1, Pallas kernels, on_device(): pl.pallas_call(functools.partial(kernel, segs, count), out_shape=(jax.Sha...  148 us

profile of v3, /device:TPU:0, one launch (start us, length us, event | category | flops | bytes accessed | tf_op | source)
XLA Modules:
  0.0 150.0 jit_solution(5868567549759182755)
XLA Ops:
  0.6 147.6 %lanczos.1 = (bf16[3,128,128]{2,1,0:T(8,128)(2,1)}, f32[3,128,128]{2,1,0:T(8,128)}, f32[1,11]{1,0:T(1,128)}) custom-call(bf16[3,128,128]{2,1,0:T(8,128)(2,1)} %bitcast.14, bf16[3,40,128,128]{3,2,1,0:T(8,128)(2,1)} %bitcast.12, bf16[3,40,128,128]{3,2,1,0:T(8,128)(2,1)} %bitcast.13, bf16[3,128,128]{2,1,0:T(8,128)(2,1)} %bitcast.15, ...), custom_call_target="tpu_custom_call" | custom-call | tf_op jit(solution)/shard_map/lanczos/pallas_call | solution.py:523
  148.3 1.7 %hand_on.1 = (bf16[3,128,128]{2,1,0:T(8,128)(2,1)}, f32[3,128,128]{2,1,0:T(8,128)}, f32[1,11]{1,0:T(1,128)}) custom-call(bf16[3,128,128]{2,1,0:T(8,128)(2,1)} %get-tuple-element.9.refs_0_, f32[3,128,128]{2,1,0:T(8,128)} %get-tuple-element.10.refs_1_, f32[1,11]{1,0:T(1,128)} %get-tuple-element.11.refs_2_), custom_call_target="tpu_custom_call" | custom-call | tf_op jit(solution)/shard_map/hand_on/pallas_call | solution.py:509

commit v4 on v3

--- a/solution.py
+++ b/solution.py
@@ -126,12 +126,12 @@
             device_id=device, device_id_type=BY_ID,
         ).start()
 
-    loads = []
-    for b in range(BLK):
-        for side, ref in ((0, env_left), (1, env_right)):
-            c = pltpu.make_async_copy(ref.at[b], env_in.at[side, b], load_sem.at[side, b])
-            c.start()
-            loads.append(c)
+    def load(side, b):
+        ref = env_left if side == 0 else env_right
+        return pltpu.make_async_copy(ref.at[b], env_in.at[side, b], load_sem.at[side, b])
+
+    for side in range(2):
+        load(side, 0).start()
 
     stats[0] = jnp.zeros((8, BD), F32)
 
@@ -182,42 +182,48 @@
 
     for t in range(BLK):
         pieces[0, t, 0, 0, :BD, :] = psi[t]
-        pieces[0, t, 0, 0, BD:, :] = jnp.zeros((TILE, BD), BF)
         own[t] = psi[t]
+    pieces[0, BLK - 1, 0, 0, BD:, :] = jnp.zeros((TILE, BD), BF)
 
     pl.semaphore_wait(
         barrier, len(PEERS) + jnp.where(seg > 0, 1, 0) + jnp.where(seg < segs - 1, 1, 0)
     )
 
-    axes = ((0, to_y, pl.ds(0, HALF)), (1, to_z, pl.ds(HALF, ROWS - HALF)))
+    def height(t):
+        return ROWS if t == BLK - 1 else BD
+
+    def axes(t):
+        return (0, to_y, pl.ds(0, HALF)), (1, to_z, pl.ds(HALF, height(t) - HALF))
 
     def direct(p, t, h):
-        return pieces.at[p, t, 0, pl.ds(1, 3)] if h == 0 else pieces.at[p, t, pl.ds(1, 3), 0]
+        rows = pl.ds(0, height(t))
+        return pieces.at[p, t, 0, pl.ds(1, 3), rows] if h == 0 else pieces.at[p, t, pl.ds(1, 3), 0, rows]
 
     def bundle(p, t, h, o, rows):
         return pieces.at[p, t, o, pl.ds(1, 3), rows] if h == 0 else pieces.at[p, t, pl.ds(1, 3), o, rows]
 
     def gather_first(p, t):
-        mine = pieces.at[p, t, 0, 0]
-        for d in (1, 3, 2):
+        rows = pl.ds(0, height(t))
+        mine = pieces.at[p, t, 0, 0, rows]
+        for d in (2, 1, 3):
             back = (4 - d) % 4
-            send(mine, pieces.at[p, t, 0, back], ssem.at[p, t, 0, 0], rsem.at[p, t, 0, 0], to_z[d])
-            send(mine, pieces.at[p, t, back, 0], ssem.at[p, t, 1, 0], rsem.at[p, t, 1, 0], to_y[d])
+            send(mine, pieces.at[p, t, 0, back, rows], ssem.at[p, t, 0, 0], rsem.at[p, t, 0, 0], to_z[d])
+            send(mine, pieces.at[p, t, back, 0, rows], ssem.at[p, t, 1, 0], rsem.at[p, t, 1, 0], to_y[d])
 
     def gather_second(p, t):
-        for h, to, rows in axes:
+        for h, to, rows in axes(t):
             wait_bytes(direct(p, t, h), rsem.at[p, t, h, 0])
-            for d in (1, 3, 2):
+            for d in (2, 1, 3):
                 back = (4 - d) % 4
                 send(bundle(p, t, h, 0, rows), bundle(p, t, h, back, rows), ssem.at[p, t, h, 1], rsem.at[p, t, h, 1], to[d])
 
     def gather_end(p, t):
-        for h, _, rows in axes:
+        for h, _, rows in axes(t):
             wait_bytes(pieces.at[p, t, pl.ds(1, 3), pl.ds(1, 3), rows], rsem.at[p, t, h, 1])
-        local[t] = pieces[p, t]
+        local[t, :, :, :height(t), :] = pieces[p, t, :, :, :height(t), :]
 
     def gather_sent(p, t):
-        for h, _, rows in axes:
+        for h, _, rows in axes(t):
             wait_bytes(direct(p, t, h), ssem.at[p, t, h, 0])
             wait_bytes(pieces.at[p, t, pl.ds(1, 3), pl.ds(1, 3), rows], ssem.at[p, t, h, 1])
 
@@ -261,6 +267,12 @@
         @pl.when(b == 0)
         def _():
             spread_mix(side, rows)
+
+        @pl.when(step == 1)
+        def _():
+            for late in range(1, BLK):
+                load(0, late).start()
+                load(1, late).start()
 
         maps = mix_kron[side, rows, :]
         for i in range(BD // (2 * TILE)):
@@ -376,20 +388,26 @@
         if final:
             leftover[t] = w
             stats[0, t:t + 1, :] = prod
-            return
+            return None
         pieces[p, t, 0, 0, :BD, :] = y.astype(BF)
+        return prod, norm, a, total(y * y)
+
+    def tell(p, found):
         row = lax.broadcasted_iota(jnp.int32, (TILE, BD), 0)
         kind = row % 4
-        value = jnp.where(kind == 0, prod, jnp.where(kind == 1, norm, jnp.where(kind == 2, a, total(y * y))))
+        pick = [jnp.where(lane < 32, x, jnp.where(lane < 64, y, z)) for x, y, z in zip(*found)]
+        value = jnp.where(kind == 0, pick[0], jnp.where(kind == 1, pick[1], jnp.where(kind == 2, pick[2], pick[3])))
         one = value.astype(BF).astype(F32)
         two = (value - one).astype(BF).astype(F32)
         three = (value - one - two).astype(BF).astype(F32)
         tile = jnp.where(row < 4, one, jnp.where(row < 8, two, jnp.where(row < 12, three, 0.0)))
-        pieces[p, t, 0, 0, BD:, :] = tile.astype(BF)
-
-    def learn(t):
-        parts = local[t, :, :, BD:, :].astype(F32).reshape(16, TILE, BD)
-        facts[t] = parts[:, 0:4, :] + parts[:, 4:8, :] + parts[:, 8:12, :]
+        pieces[p, BLK - 1, 0, 0, BD:, :] = tile.astype(BF)
+
+    def learn():
+        parts = local[BLK - 1, :, :, BD:, :].astype(F32).reshape(16, TILE, BD)
+        value = parts[:, 0:4, :] + parts[:, 4:8, :] + parts[:, 8:12, :]
+        for t in range(BLK):
+            facts[t] = jnp.broadcast_to(value[:, :, 32 * t:32 * t + 1], (16, 4, BD))
 
     def scalars():
         alpha = jnp.zeros((1, BD), F32)
@@ -416,6 +434,7 @@
 
     image[...] = jnp.zeros_like(image)
 
+    found = []
     for b in range(BLK):
         def apply_first(c, _, b=b):
             @pl.when(seg > 0)
@@ -430,7 +449,9 @@
             return 0
 
         lax.fori_loop(0, CHUNKS, apply_first, 0)
-        finish(1, b, image[b], sigma0, None)
+        found.append(finish(1, b, image[b], sigma0, None))
+        if b == BLK - 1:
+            tell(1, found)
         gather_first(1, b)
         gather_onward(1, b)
 
@@ -439,7 +460,9 @@
         p = (k + 1) % 2
         for t in range(BLK):
             gather_end(last, t)
-            learn(t)
+            if t < BLK - 1:
+                gather_sent(last, t)
+        learn()
         alpha, beta = scalars()
         coefs = jnp.where(lane == 2 * k - 2, alpha, coefs)
         coefs = jnp.where(lane == 2 * k - 1, beta, coefs)
@@ -453,6 +476,7 @@
             return 0
 
         one = jnp.ones((1, BD), F32)
+        found = []
         for t in range(BLK):
             lax.fori_loop(t * ENT, (t + 1) * ENT, correct, 0, unroll=True)
             gap = (alpha - facts[t, 0, 2:3, :]) * sigma
@@ -460,11 +484,12 @@
             before[t] = v * sigma
             own[t] = ((local[t, 0, 0, :BD, :].astype(F32) - gap * v) * inverse).astype(BF)
             combine(t)
-            finish(p, t, contract(t, 0, CH), one, beta, final)
+            found.append(finish(p, t, contract(t, 0, CH), one, beta, final))
             if t == 0:
-                for u in range(BLK):
-                    gather_sent(last, u)
+                gather_sent(last, BLK - 1)
             if not final:
+                if t == BLK - 1:
+                    tell(p, found)
                 gather_first(p, t)
                 gather_onward(p, t)
         return coefs

time: 152 us -> 147 us (0.967)
  Pallas kernels: 149 us -> 145 us
    pallas_call x1, Pallas kernels: 148 us -> 143 us  [on_device(): pl.pallas_call(functools.partial(kernel, segs, count), out_shape=(jax.Sha...]
where the time goes in v4:
time: 147 us; the launch traced here: 145 us
  Pallas kernels  145 us (99%)
    pallas_call x1, Pallas kernels, on_device(): pl.pallas_call(functools.partial(kernel, segs, count), out_shape=(jax.Sha...  143 us

profile of v4, /device:TPU:0, one launch (start us, length us, event | category | flops | bytes accessed | tf_op | source)
XLA Modules:
  0.0 145.4 jit_solution(9569584799788341393)
XLA Ops:
  0.6 143.0 %lanczos.1 = (bf16[3,128,128]{2,1,0:T(8,128)(2,1)}, f32[3,128,128]{2,1,0:T(8,128)}, f32[1,11]{1,0:T(1,128)}) custom-call(bf16[3,128,128]{2,1,0:T(8,128)(2,1)} %bitcast.14, bf16[3,40,128,128]{3,2,1,0:T(8,128)(2,1)} %bitcast.12, bf16[3,40,128,128]{3,2,1,0:T(8,128)(2,1)} %bitcast.13, bf16[3,128,128]{2,1,0:T(8,128)(2,1)} %bitcast.15, ...), custom_call_target="tpu_custom_call" | custom-call | tf_op jit(solution)/shard_map/lanczos/pallas_call | solution.py:548
  143.6 1.7 %hand_on.1 = (bf16[3,128,128]{2,1,0:T(8,128)(2,1)}, f32[3,128,128]{2,1,0:T(8,128)}, f32[1,11]{1,0:T(1,128)}) custom-call(bf16[3,128,128]{2,1,0:T(8,128)(2,1)} %get-tuple-element.9.refs_0_, f32[3,128,128]{2,1,0:T(8,128)} %get-tuple-element.10.refs_1_, f32[1,11]{1,0:T(1,128)} %get-tuple-element.11.refs_2_), custom_call_target="tpu_custom_call" | custom-call | tf_op jit(solution)/shard_map/hand_on/pallas_call | solution.py:534

commit v5 on v4

--- a/solution.py
+++ b/solution.py
@@ -210,7 +210,21 @@
             send(mine, pieces.at[p, t, 0, back, rows], ssem.at[p, t, 0, 0], rsem.at[p, t, 0, 0], to_z[d])
             send(mine, pieces.at[p, t, back, 0, rows], ssem.at[p, t, 1, 0], rsem.at[p, t, 1, 0], to_y[d])
 
+    def both(p, h, o, rows):
+        ts = pl.ds(0, 2)
+        return pieces.at[p, ts, o, pl.ds(1, 3), rows] if h == 0 else pieces.at[p, ts, pl.ds(1, 3), o, rows]
+
     def gather_second(p, t):
+        if t == 0:
+            return
+        if t == 1:
+            for h, to, rows in axes(t):
+                wait_bytes(direct(p, 0, h), rsem.at[p, 0, h, 0])
+                wait_bytes(direct(p, 1, h), rsem.at[p, 1, h, 0])
+                for d in (2, 1, 3):
+                    back = (4 - d) % 4
+                    send(both(p, h, 0, rows), both(p, h, back, rows), ssem.at[p, t, h, 1], rsem.at[p, t, h, 1], to[d])
+            return
         for h, to, rows in axes(t):
             wait_bytes(direct(p, t, h), rsem.at[p, t, h, 0])
             for d in (2, 1, 3):
@@ -219,13 +233,19 @@
 
     def gather_end(p, t):
         for h, _, rows in axes(t):
-            wait_bytes(pieces.at[p, t, pl.ds(1, 3), pl.ds(1, 3), rows], rsem.at[p, t, h, 1])
+            if t == 0:
+                wait_bytes(pieces.at[p, pl.ds(0, 2), pl.ds(1, 3), pl.ds(1, 3), rows], rsem.at[p, 1, h, 1])
+            if t == 2:
+                wait_bytes(pieces.at[p, t, pl.ds(1, 3), pl.ds(1, 3), rows], rsem.at[p, t, h, 1])
         local[t, :, :, :height(t), :] = pieces[p, t, :, :, :height(t), :]
 
     def gather_sent(p, t):
         for h, _, rows in axes(t):
             wait_bytes(direct(p, t, h), ssem.at[p, t, h, 0])
-            wait_bytes(pieces.at[p, t, pl.ds(1, 3), pl.ds(1, 3), rows], ssem.at[p, t, h, 1])
+            if t == 0:
+                wait_bytes(pieces.at[p, pl.ds(0, 2), pl.ds(1, 3), pl.ds(1, 3), rows], ssem.at[p, 1, h, 1])
+            if t == 2:
+                wait_bytes(pieces.at[p, t, pl.ds(1, 3), pl.ds(1, 3), rows], ssem.at[p, t, h, 1])
 
     def gather_onward(p, t):
         if t > 0:

time: 147 us -> 147 us (level)
  no operation moved by 1% of the time
where the time goes in v5:
time: 147 us; the launch traced here: 144 us
  Pallas kernels  144 us (98%)
    pallas_call x1, Pallas kernels, on_device(): pl.pallas_call(functools.partial(kernel, segs, count), out_shape=(jax.Sha...  142 us

profile of v5, /device:TPU:0, one launch (start us, length us, event | category | flops | bytes accessed | tf_op | source)
XLA Modules:
  0.0 144.2 jit_solution(2272995190403931248)
XLA Ops:
  0.6 141.9 %lanczos.1 = (bf16[3,128,128]{2,1,0:T(8,128)(2,1)}, f32[3,128,128]{2,1,0:T(8,128)}, f32[1,11]{1,0:T(1,128)}) custom-call(bf16[3,128,128]{2,1,0:T(8,128)(2,1)} %bitcast.14, bf16[3,40,128,128]{3,2,1,0:T(8,128)(2,1)} %bitcast.12, bf16[3,40,128,128]{3,2,1,0:T(8,128)(2,1)} %bitcast.13, bf16[3,128,128]{2,1,0:T(8,128)(2,1)} %bitcast.15, ...), custom_call_target="tpu_custom_call" | custom-call | tf_op jit(solution)/shard_map/lanczos/pallas_call | solution.py:568
  142.5 1.7 %hand_on.1 = (bf16[3,128,128]{2,1,0:T(8,128)(2,1)}, f32[3,128,128]{2,1,0:T(8,128)}, f32[1,11]{1,0:T(1,128)}) custom-call(bf16[3,128,128]{2,1,0:T(8,128)(2,1)} %get-tuple-element.9.refs_0_, f32[3,128,128]{2,1,0:T(8,128)} %get-tuple-element.10.refs_1_, f32[1,11]{1,0:T(1,128)} %get-tuple-element.11.refs_2_), custom_call_target="tpu_custom_call" | custom-call | tf_op jit(solution)/shard_map/hand_on/pallas_call | solution.py:554
